TPU v7x, 256 devices: a whole 4x4x8 slice. The times are simulated.
256 devices in a mesh: unit: 64 (over y, z, core), vec: 4 (over x).
Axes of the slice: x: 4, y: 4, z: 8, core: 2. Of those that a mesh axis runs over, the one named last changes fastest.
Arguments:
- tangents: bfloat16 [262144, 512], P('unit', 'vec'), may hold values from -120 to 120, as said below
- state: float32 [262144], P('unit'), may hold values from -6 to 6
- gain: float32 [262144], P('unit'), may hold values from 0.8 to 3
- local_w: bfloat16 [16384, 128, 128], P('unit'), may hold values from -0.15625 to 0.15625
- local_row: int32 [16384], P('unit'), may hold values from 0 to 31
- local_col: int32 [16384], P('unit'), may hold values from 0 to 31
- remote_w: bfloat16 [4096, 128, 128], P('unit'), may hold values from -0.15625 to 0.15625
- remote_row: int32 [4096], P('unit'), may hold values from 0 to 31
- remote_owner: int32 [4096, 1], P('unit'), may hold values from 0 to 63; in each aligned block of 64 rows (0 to 63, 64 to 127, ...) at most 2 rows name the same one
- remote_offset: int32 [4096], P('unit'), may hold values from 0 to 31
Outputs:
- new_tangents: bfloat16 [262144, 512], P('unit', 'vec')
- exponents: float32 [512], replicated
Inputs may be any that keep to these rules, and one draw needn't show every extreme that they name: `tangents`: the 512 columns are linearly independent. `remote_owner`: among the 64 second-part blocks of one shard no owner is named more than 2 times, a bound that some block reaches.
All inputs are finite; a program needn't handle non-finite values.
Results may differ from a plain program's by a relative error of at most 0.003.
The roundings to bfloat16 on the way count: a program that leaves them out, or rounds other values in their place, can miss the bound.
Values may be sent and summed in bfloat16 or wider, within the bound.
No kernel may reach another device: no remote copies, remote signals or barrier semaphores. Data moves between devices by JAX's collectives and lax.ppermute only.
A program may use at most 128 MiB of HBM per device.

v0:
```python
import jax
import jax.numpy as jnp
from jax import lax
from jax.sharding import PartitionSpec as P

time_step = 0.5


def cholesky_parts(gram_matrix):
    lower_factor = jnp.linalg.cholesky(gram_matrix)
    identity_m = jnp.eye(gram_matrix.shape[0], dtype=jnp.float32)
    inverse_low = jax.scipy.linalg.solve_triangular(lower_factor, identity_m, lower=True)
    return (inverse_low.T.astype(jnp.bfloat16), jnp.log(jnp.diagonal(lower_factor)))


def body(
    tangents,
    state,
    gain,
    local_w,
    local_row,
    local_col,
    remote_w,
    remote_row,
    remote_owner,
    remote_offset,
):
    rows_dev, width_dev = tangents.shape
    block_side = local_w.shape[1]
    block_rows = rows_dev // block_side
    unit_count = lax.axis_size("unit")
    unit_total = float(rows_dev * unit_count)
    slopes = gain * (1.0 - jnp.tanh(gain * state) ** 2)
    scaled = (slopes[:, None] * tangents.astype(jnp.float32)).astype(jnp.bfloat16)
    pieces = scaled.reshape(block_rows, block_side, width_dev)
    owners = remote_owner[:, 0]
    far_count = owners.shape[0]
    capacity = max(2, 2 * far_count // unit_count)
    positions = jnp.arange(far_count, dtype=jnp.int32)
    earlier_same = (owners[:, None] == owners[None, :]) & (positions[None, :] < positions[:, None])
    slot_rank = jnp.sum(earlier_same.astype(jnp.int32), axis=1)
    targets = owners * capacity + slot_rank
    all_slots = jnp.arange(unit_count * capacity, dtype=jnp.int32)
    matches = targets[:, None] == all_slots[None, :]
    wanted = jnp.sum(jnp.where(matches, remote_offset[:, None], 0), axis=0).reshape(
        unit_count, capacity
    )
    chosen = pieces[lax.all_to_all(wanted, "unit", split_axis=0, concat_axis=0, tiled=True)]
    arrived = lax.all_to_all(chosen, "unit", split_axis=0, concat_axis=0, tiled=True)
    near_blocks = pieces[local_col]
    local_terms = jnp.einsum(
        "bij,bjk->bik", local_w, near_blocks, preferred_element_type=jnp.float32
    )
    local_sum = jax.ops.segment_sum(local_terms, local_row, num_segments=block_rows)
    far_blocks = arrived.reshape(unit_count * capacity, block_side, width_dev)[targets]
    far_terms = jnp.einsum("bij,bjk->bik", remote_w, far_blocks, preferred_element_type=jnp.float32)
    far_sum = jax.ops.segment_sum(far_terms, remote_row, num_segments=block_rows)
    coupled = (local_sum + far_sum).reshape(rows_dev, width_dev)
    stepped = ((1.0 - time_step) * tangents.astype(jnp.float32) + time_step * coupled).astype(
        jnp.bfloat16
    )
    row_part = lax.all_to_all(stepped, "vec", split_axis=0, concat_axis=1, tiled=True)
    partial_gram = jnp.einsum("ra,rb->ab", row_part, row_part, preferred_element_type=jnp.float32)
    gram_matrix = lax.psum(partial_gram, ("unit", "vec")) / unit_total
    inverse_up, exponents = cholesky_parts(gram_matrix)
    renewed_rows = jnp.dot(row_part, inverse_up, preferred_element_type=jnp.float32).astype(
        jnp.bfloat16
    )
    renewed = lax.all_to_all(renewed_rows, "vec", split_axis=1, concat_axis=0, tiled=True)
    return (renewed, exponents)


def solution(mesh):
    placed = (
        P("unit", "vec"),
        P("unit"),
        P("unit"),
        P("unit", None, None),
        P("unit"),
        P("unit"),
        P("unit", None, None),
        P("unit"),
        P("unit", None),
        P("unit"),
    )
    return jax.shard_map(
        body, mesh=mesh, in_specs=placed, out_specs=(P("unit", "vec"), P()), check_vma=False
    )
```

profile of v0, /device:TPU:1, one launch (start us, length us, event | category | flops | bytes accessed | tf_op | source)
XLA Modules:
  0.0 631.4 jit_solution(7501308896463806125)
XLA Ops:
  10.4 13.2 %all-to-all-start = ((s32[64,1,2]{2,1,0:T(1,128)}), s32[64,1,2]{2,1,0:T(1,128)S(1)}, u32[]{:S(2)}, u32[]{:S(2)}) async-start(s32[64,1,2]{2,1,0:T(1,128)} %bitcast.5), calls=%async_computation | async-start | bytes 65536 | tf_op jit(solution)/shard_map/all_to_all | solution.py:48
  26.0 6.7 %all-to-all-done = s32[64,1,2]{2,1,0:T(1,128)S(1)} async-done(((s32[64,1,2]{2,1,0:T(1,128)}), s32[64,1,2]{2,1,0:T(1,128)S(1)}, u32[]{:S(2)}, u32[]{:S(2)}) %all-to-all-start) | async-done | bytes 544 | tf_op jit(solution)/shard_map/all_to_all | solution.py:48
  33.1 3.0 gather_fusion.1
  36.1 5.8 all-to-all-start.1
  42.5 8.6 %gather_fusion = bf16[256,128,128]{2,1,0:T(8,128)(2,1)} fusion(bf16[32,128,128]{2,1,0:T(8,128)(2,1)S(1)} %bitcast.94, s32[1024]{0:T(1024)S(1)} %pad_clamp_fusion.2), kind=kCustom, calls=%fused_computation | custom fusion | bytes 16778240 | tf_op jit(solution)/shard_map/gather | solution.py:50
  51.1 12.8 %convolution_bitcast_fusion = f32[256,128,128]{1,2,0:T(8,128)} fusion(bf16[256,128,128]{2,1,0:T(8,128)(2,1)} %gather_fusion, bf16[256,128,128]{2,1,0:T(8,128)(2,1)} %param.13), kind=kOutput, calls=%fused_computation.8 | convolution fusion | flops 1073741824 | bytes 33554432 | tf_op jit(solution)/shard_map/bij,bjk->bik/dot_general | solution.py:51
  64.0 17.5 %copy.50 = f32[256,128,128]{2,1,0:T(8,128)} copy(f32[256,128,128]{1,2,0:T(8,128)} %convolution_bitcast_fusion) | data formatting | bytes 33554432 | tf_op jit(solution)/shard_map/bij,bjk->bik/dot_general | solution.py:51
  83.0 51.3 %scatter_fusion = f32[32,128,128]{2,1,0:T(8,128)} fusion(f32[32,128,128]{2,1,0:T(8,128)} %broadcast.217.clone, s32[256]{0:T(256)S(1)} %copy-done.6, f32[256,128,128]{2,1,0:T(8,128)} %copy.50), kind=kCustom, calls=%fused_computation.4 | custom fusion | flops 4194304 | bytes 50332672 | tf_op jit(solution)/shard_map/scatter-add | solution.py:54
  134.3 3.5 all-to-all-done.1
  137.9 4.4 gather_fusion.2
  142.2 5.2 convolution_bitcast_fusion.1
  147.4 5.6 copy.55
  154.6 13.4 %scatter_fusion.1 = f32[32,128,128]{2,1,0:T(8,128)} fusion(f32[32,128,128]{2,1,0:T(8,128)} %broadcast.217.clone.1, s32[64]{0:T(128)S(1)} %copy-done.8, f32[64,128,128]{2,1,0:T(8,128)} %copy.55), kind=kCustom, calls=%fused_computation.5 | custom fusion | flops 1048576 | bytes 12583168 | tf_op jit(solution)/shard_map/scatter-add | solution.py:57
  170.9 18.1 %all_to_all.55 = bf16[4,1024,128]{2,1,0:T(8,128)(2,1)S(1)} all-to-all(bf16[4,1024,128]{2,1,0:T(8,128)(2,1)S(1)} %bitcast.98), channel_id=1, replica_groups=mesh['unit'=64,'vec'=4] {'vec'}, dimensions={0} | all-to-all | bytes 2097152 | tf_op jit(solution)/shard_map/all_to_all | solution.py:62
  190.4 3.3 fusion.49
  195.6 249.7 %all-reduce.3.cloned.1.call-done = f32[512,512]{0,1:T(8,128)} async-done(((f32[512,512]{0,1:T(8,128)}), f32[512,512]{0,1:T(8,128)}) %all-reduce.3.cloned.1.call-update) | async-done | bytes 1048592 | tf_op jit(solution)/shard_map/psum | solution.py:64
  452.8 11.7 %cholesky.104 = f32[128,128]{1,0:T(8,128)S(1)} custom-call(f32[128,128]{1,0:T(8,128)S(1)} %cholesky.266), custom_call_target="Cholesky" | custom-call | tf_op jit(solution)/shard_map/jit(cholesky)/cholesky | solution.py:10
  464.5 9.8 %custom-call.31 = f32[1,128,128]{1,2,0:T(8,128)S(1)} custom-call(f32[1,128,128]{2,1,0:T(8,128)S(1)} %get-tuple-element.31), custom_call_target="InvertDiagBlocksLowerTriangular" | custom-call | tf_op jit(solution)/shard_map/jit(cholesky)/cholesky | solution.py:10
  477.0 11.7 %cholesky.217 = f32[128,128]{1,0:T(8,128)S(1)} custom-call(f32[128,128]{1,0:T(8,128)S(1)} %cholesky.270), custom_call_target="Cholesky" | custom-call | tf_op jit(solution)/shard_map/jit(cholesky)/cholesky | solution.py:10
  488.8 10.0 %custom-call.32 = f32[1,128,128]{1,2,0:T(8,128)S(1)} custom-call(f32[1,128,128]{2,1,0:T(8,128)S(1)} %get-tuple-element.28), custom_call_target="InvertDiagBlocksLowerTriangular" | custom-call | tf_op jit(solution)/shard_map/jit(cholesky)/cholesky | solution.py:10
  500.3 11.7 %cholesky.238 = f32[128,128]{1,0:T(8,128)S(1)} custom-call(f32[128,128]{1,0:T(8,128)S(1)} %cholesky.275), custom_call_target="Cholesky" | custom-call | tf_op jit(solution)/shard_map/jit(cholesky)/cholesky | solution.py:10
  512.7 9.8 %custom-call.33 = f32[1,128,128]{1,2,0:T(8,128)S(1)} custom-call(f32[1,128,128]{2,1,0:T(8,128)S(1)} %get-tuple-element.25), custom_call_target="InvertDiagBlocksLowerTriangular" | custom-call | tf_op jit(solution)/shard_map/jit(cholesky)/cholesky | solution.py:10
  523.9 11.9 %cholesky.255 = f32[128,128]{1,0:T(8,128)S(1)} custom-call(f32[128,128]{1,0:T(8,128)S(1)} %convolution_subtract_fusion.5), custom_call_target="Cholesky" | custom-call | tf_op jit(solution)/shard_map/jit(cholesky)/cholesky | solution.py:10
  542.2 13.8 %while.1 = (s32[]{:T(128)}, f32[512,512]{1,0:T(8,128)}, s32[4,2]{0,1:T(2,128)S(1)}, f32[4,128,128]{2,1,0:T(8,128)}, s32[]{:T(128)}) while((s32[]{:T(128)}, f32[512,512]{1,0:T(8,128)}, s32[4,2]{0,1:T(2,128)S(1)}, f32[4,128,128]{2,1,0:T(8,128)}, s32[]{:T(128)}) %tuple.36), condition=%wide.while_cond, body=%wide.while_body.sunk | while | flops 2 | bytes 132705 | solution.py:12
  542.9 2.8 bitcast_dynamic-update-slice_fusion.2
  546.3 2.8 bitcast_dynamic-update-slice_fusion.2
  549.8 2.8 bitcast_dynamic-update-slice_fusion.2
  553.3 2.8 bitcast_dynamic-update-slice_fusion.2
  556.0 40.1 %custom-call.34 = f32[4,128,128]{1,2,0:T(8,128)S(1)} custom-call(f32[4,128,128]{2,1,0:T(8,128)} %get-tuple-element.9), custom_call_target="InvertDiagBlocksLowerTriangular" | custom-call | tf_op jit(solution)/shard_map/jit(_solve_triangular)/triangular_solve | solution.py:12
  604.9 4.2 all-to-all-start.3
  609.1 4.5 gather_fusion.3
  614.2 7.8 %all-to-all-done.3 = bf16[1024,4,128]{0,2,1:T(8,128)(2,1)} async-done(((bf16[1024,4,128]{0,2,1:T(8,128)(2,1)}), bf16[1024,4,128]{0,2,1:T(8,128)(2,1)}, u32[]{:S(2)}, u32[]{:S(2)}) %all-to-all-start.3) | async-done | bytes 1048608 | tf_op jit(solution)/shard_map/all_to_all | solution.py:69
  (84 shorter events, 47.6 us)
Async XLA Ops:
  7.2 135.1 %copy-start = (bf16[64,128,128]{2,1,0:T(8,128)(2,1)S(1)}, bf16[64,128,128]{2,1,0:T(8,128)(2,1)}, u32[]{:S(2)}) copy-start(bf16[64,128,128]{2,1,0:T(8,128)(2,1)} %param.16) | copy-start | bytes 6291460
  10.4 22.4 %all-to-all-start = ((s32[64,1,2]{2,1,0:T(1,128)}), s32[64,1,2]{2,1,0:T(1,128)S(1)}, u32[]{:S(2)}, u32[]{:S(2)}) async-start(s32[64,1,2]{2,1,0:T(1,128)} %bitcast.5), calls=%async_computation | async-start | bytes 65536 | tf_op jit(solution)/shard_map/all_to_all | solution.py:48
  36.1 6.4 %copy-start.7 = (s32[256]{0:T(256)S(1)}, s32[256]{0:T(256)}, u32[]{:S(2)}) copy-start(s32[256]{0:T(256)} %param.15) | copy-start | bytes 3076
  36.1 101.8 %all-to-all-start.1 = ((bf16[64,2,128,128]{3,2,1,0:T(8,128)(2,1)}), bf16[64,2,128,128]{3,2,1,0:T(8,128)(2,1)}, u32[]{:S(2)}, u32[]{:S(2)}) async-start(bf16[64,2,128,128]{3,2,1,0:T(8,128)(2,1)} %bitcast.96), calls=%async_computation.1 | async-start | bytes 8388608 | tf_op jit(solution)/shard_map/all_to_all | solution.py:49
  41.9 403.4 %all-reduce.3.cloned.1.call-start = ((), (), s32[]{:S(2)}) async-start(), calls=%async_computation.4 | async-start | bytes 2097152 | tf_op jit(solution)/shard_map/psum | solution.py:64
  64.0 19.1 %copy-start.6 = (s32[256]{0:T(256)S(1)}, s32[256]{0:T(256)}, u32[]{:S(2)}) copy-start(s32[256]{0:T(256)} %param.14) | copy-start | bytes 3076
  147.4 7.2 %copy-start.8 = (s32[64]{0:T(128)S(1)}, s32[64]{0:T(128)}, u32[]{:S(2)}) copy-start(s32[64]{0:T(128)} %param.17) | copy-start | bytes 772
  168.0 2.6 copy-start.3
  445.3 4.9 copy-start.2
  451.7 1.0 copy-start.4
  535.9 3.9 copy-start.1
  596.2 7.0 %copy-start.5 = (bf16[1024,4,128]{0,2,1:T(8,128)(2,1)S(1)}, bf16[1024,4,128]{0,2,1:T(8,128)(2,1)}, u32[]{:S(2)}) copy-start(bf16[1024,4,128]{0,2,1:T(8,128)(2,1)} %copy.56) | copy-start | bytes 3145732
  604.9 17.2 %all-to-all-start.3 = ((bf16[1024,4,128]{0,2,1:T(8,128)(2,1)}), bf16[1024,4,128]{0,2,1:T(8,128)(2,1)}, u32[]{:S(2)}, u32[]{:S(2)}) async-start(bf16[1024,4,128]{0,2,1:T(8,128)(2,1)} %bitcast.101), calls=%async_computation.3 | async-start | bytes 2097152 | tf_op jit(solution)/shard_map/all_to_all | solution.py:69
Sparse Core Ops, SparseCore 0:
  193.9 251.4 all-reduce.2
where the time goes:
time: 638 us; the launch traced here: 631 us
  waiting for transfers between devices  268 us (42%)
  other arithmetic  200 us (31%)
  local copies, waits for them, and re-layouts  69.7 us (11%)
  matrix products  35.4 us (6%)
  starting transfers between devices  23.8 us (4%)
  blocking collectives  18.1 us (3%)
  between operations  17.1 us (3%)
    psum x1, waiting for transfers between devices, body(): gram_matrix = lax.psum(partial_gram, ('unit', 'vec')) / unit_total  250 us
    another operation x14, other arithmetic, cholesky_parts(): lower_factor = jnp.linalg.cholesky(gram_matrix)  78.9 us
    scatter-add x1, other arithmetic, body(): jax.ops.segment_sum(local_terms, local_row, num_segments=block_rows)  51.3 us
    another operation x3, other arithmetic, cholesky_parts(): jax.scipy.linalg.solve_triangular(lower_factor, identity_m, lower=True)  42.5 us
    all_to_all x1, blocking collectives, body(): lax.all_to_all(stepped, 'vec', split_axis=0, concat_axis=1, tiled=True)  18.1 us
    dot_general x1, local copies, waits for them, and re-layouts, body(): jnp.einsum('bij,bjk->bik', local_w, near_blocks, preferred_element_type=j...  17.5 us
    another operation x14, local copies, waits for them, and re-layouts  16.9 us
    scatter-add x1, other arithmetic, body(): jax.ops.segment_sum(far_terms, remote_row, num_segments=block_rows)  13.4 us
  transfers between devices with their start and end apart: 4, of which 4 were waited for; matrix products, arithmetic and copies ran while one was open for 16% of the time, Pallas kernels for 0%

commit v1 on v0

v1 whole, which is shorter than its diff:
```python
import functools

import jax
import jax.numpy as jnp
from jax import lax
from jax.experimental import pallas as pl
from jax.experimental.pallas import tpu as pltpu
from jax.sharding import PartitionSpec as P

time_step = 0.5
HIGHEST = lax.Precision.HIGHEST
MIB = 1024 * 1024


def split_dot(left, right, left_dim, right_dim):
    return lax.dot_general(
        left,
        right,
        (((left_dim,), (right_dim,)), ((), ())),
        precision=HIGHEST,
        preferred_element_type=jnp.float32,
    )


def local_kernel(row_ref, col_ref, w_ref, x_ref, t_ref, acc_ref):
    step = pl.program_id(0)
    count = w_ref.shape[0]

    @pl.when(step == 0)
    def _():
        acc_ref[...] = t_ref[...].astype(jnp.float32)

    @pl.loop(0, count // 8)
    def _(group):
        for inner in range(8):
            block = group * 8 + inner
            row = row_ref[step * count + block]
            col = col_ref[step * count + block]
            acc_ref[row] += jnp.dot(w_ref[block], x_ref[col], preferred_element_type=jnp.float32)


def local_product(local_row, local_col, local_w, pieces, tangents):
    count, side, _ = local_w.shape
    block_rows, _, width = pieces.shape
    chunk = 32
    whole = lambda i, *_: (0, 0, 0)
    return pl.pallas_call(
        local_kernel,
        grid_spec=pltpu.PrefetchScalarGridSpec(
            num_scalar_prefetch=2,
            grid=(count // chunk,),
            in_specs=[
                pl.BlockSpec((chunk, side, side), lambda i, *_: (i, 0, 0)),
                pl.BlockSpec((block_rows, side, width), whole),
                pl.BlockSpec((block_rows, side, width), whole),
            ],
            out_specs=pl.BlockSpec((block_rows, side, width), whole),
        ),
        out_shape=jax.ShapeDtypeStruct((block_rows, side, width), jnp.float32),
        compiler_params=pltpu.CompilerParams(vmem_limit_bytes=16 * MIB),
        cost_estimate=pl.CostEstimate(
            flops=2 * count * side * side * width, bytes_accessed=14 * MIB, transcendentals=0
        ),
        name="local_blocks",
    )(local_row, local_col, local_w, pieces, tangents)


def column_of(row, side):
    return jnp.broadcast_to(row, (side, side)).T


def spread_kernel(state_ref, gain_ref, t_ref, ask_ref, pieces_ref, spread_ref):
    block_rows, side, width = t_ref.shape
    half = side // 2
    gain = gain_ref[...]
    slopes = gain * (1.0 - jnp.tanh(gain * state_ref[...]) ** 2)
    for p in range(block_rows):
        slope = column_of(slopes[p : p + 1, :], side)
        pieces_ref[p] = (slope * t_ref[p].astype(jnp.float32)).astype(jnp.bfloat16)
    for h in range(2):
        for g in range(block_rows // 16):
            group = pieces_ref[16 * g : 16 * g + 16, h * half : (h + 1) * half, :]
            at = h * block_rows + 16 * g
            spread_ref[:, at : at + 16, :] = jnp.swapaxes(group, 0, 1)
    units, rows, _ = spread_ref.shape
    extra = rows - 2 * block_rows
    spread_ref[:, 2 * block_rows :, :] = jnp.broadcast_to(
        ask_ref[...].reshape(1, 1, width), (units, extra, width)
    )


def spread_pieces(state, gain, blocks, ask, units):
    block_rows, side, width = blocks.shape
    rows = 2 * block_rows + 8
    vmem = pl.BlockSpec(memory_space=pltpu.VMEM)
    return pl.pallas_call(
        spread_kernel,
        in_specs=[vmem] * 4,
        out_specs=[vmem] * 2,
        out_shape=[
            jax.ShapeDtypeStruct((block_rows, side, width), jnp.bfloat16),
            jax.ShapeDtypeStruct((units, rows, width), jnp.bfloat16),
        ],
        compiler_params=pltpu.CompilerParams(vmem_limit_bytes=16 * MIB),
        cost_estimate=pl.CostEstimate(
            flops=4 * MIB, bytes_accessed=4 * MIB, transcendentals=block_rows * side
        ),
        name="spread_pieces",
    )(state.reshape(block_rows, side), gain.reshape(block_rows, side), blocks, ask)


def pick_kernel(block_rows, index_ref, table_ref, out_ref):
    shards, rows, width = out_ref.shape
    owners = table_ref.shape[0]
    depth = owners * block_rows
    table = jnp.concatenate(
        [
            table_ref[:, h * block_rows : (h + 1) * block_rows, :].reshape(depth, width)
            for h in range(2)
        ],
        axis=1,
    )
    index = jnp.concatenate(
        [column_of(index_ref[0, g : g + 1, :], width) for g in range(index_ref.shape[1])], axis=0
    ).astype(jnp.int32)
    lane = lax.broadcasted_iota(jnp.int32, index.shape, 1)
    hot = jnp.concatenate(
        [(index == lane + width * k).astype(jnp.bfloat16) for k in range(depth // width)], axis=1
    )
    found = jnp.dot(hot, table, preferred_element_type=jnp.float32).astype(jnp.bfloat16)
    found = found.reshape(shards, rows // 2, 2 * width)
    out_ref[:, : rows // 2, :] = found[:, :, :width]
    out_ref[:, rows // 2 :, :] = found[:, :, width:]


def pick_rows(index, table, block_rows):
    units, far_count = index.shape
    width = table.shape[-1]
    steps = 4
    lines = units * far_count // width // steps
    return pl.pallas_call(
        functools.partial(pick_kernel, block_rows),
        grid=(steps,),
        in_specs=[
            pl.BlockSpec((1, lines, width), lambda i: (i, 0, 0)),
            pl.BlockSpec(table.shape, lambda i: (0, 0, 0)),
        ],
        out_specs=pl.BlockSpec((units // steps, 2 * far_count, width), lambda i: (i, 0, 0)),
        out_shape=jax.ShapeDtypeStruct((units, 2 * far_count, width), jnp.bfloat16),
        compiler_params=pltpu.CompilerParams(vmem_limit_bytes=32 * MIB),
        cost_estimate=pl.CostEstimate(
            flops=4_000_000_000, bytes_accessed=4 * MIB, transcendentals=0
        ),
        name="pick_rows",
    )(index.reshape(steps, lines, width), table)


def far_kernel(own_ref, row_ref, w_ref, acc_in_ref, arrived_ref, out_ref, *rest):
    part_refs, (acc_ref, x_ref) = rest[:-2], rest[-2:]
    count = w_ref.shape[0]
    units = arrived_ref.shape[0]
    acc_ref[...] = acc_in_ref[...]
    for g in range(count // 16):
        for h in range(2):
            at = h * count + 16 * g
            x_ref[16 * g : 16 * g + 16, h * units : (h + 1) * units, :] = jnp.swapaxes(
                arrived_ref[:, at : at + 16, :], 0, 1
            )
        for inner in range(16):
            block = 16 * g + inner
            row = row_ref[block]
            acc_ref[row] += jnp.dot(w_ref[block], x_ref[block], preferred_element_type=jnp.float32)
    out_ref[...] = (time_step * acc_ref[...]).astype(jnp.bfloat16)
    parts = len(part_refs)
    for k in range(parts):
        share = part_refs[k].shape[0]
        part_refs[k][...] = out_ref[pl.ds(lax.rem(own_ref[0] + k, parts) * share, share)]


def far_product(own, remote_row, remote_w, acc, arrived, parts):
    count, side, _ = remote_w.shape
    block_rows, _, width = acc.shape
    vmem = pl.BlockSpec(memory_space=pltpu.VMEM)
    return pl.pallas_call(
        far_kernel,
        in_specs=[pl.BlockSpec(memory_space=pltpu.SMEM)] * 2 + [vmem] * 3,
        out_specs=[vmem] * (1 + parts),
        out_shape=[jax.ShapeDtypeStruct((block_rows, side, width), jnp.bfloat16)]
        + [jax.ShapeDtypeStruct((block_rows // parts, side, width), jnp.bfloat16)] * parts,
        scratch_shapes=[
            pltpu.VMEM((block_rows, side, width), jnp.float32),
            pltpu.VMEM((count, side, width), jnp.bfloat16),
        ],
        compiler_params=pltpu.CompilerParams(vmem_limit_bytes=20 * MIB),
        cost_estimate=pl.CostEstimate(
            flops=2 * count * side * side * width, bytes_accessed=8 * MIB, transcendentals=0
        ),
        name="far_blocks",
    )(own, remote_row, remote_w, acc, arrived)


def cross(left, right):
    return lax.dot_general(
        left, right, (((0,), (0,)), ((), ())), preferred_element_type=jnp.float32
    )


def gram_kernel(own_ref, *refs):
    parts = len(refs) // 2
    x_refs, out_refs = refs[:parts], refs[parts:]
    side = x_refs[0].shape[1]
    half = side // 2
    for k in range(parts):
        device = lax.rem(own_ref[0] + k, parts)
        here, after, across = (x_refs[(-k - step) % parts][...] for step in (0, 1, 2))
        products = cross(here, jnp.concatenate([here, after, across], axis=1))
        out_refs[k][:side, :] = products[:, :side]
        out_refs[k][side : 2 * side, :] = products[:, side : 2 * side]
        last = products[:, 2 * side :]
        out_refs[k][2 * side :, :] = jnp.where(device < 2, last[:half], last.T[half:])


def gram_quarters(own, row_parts):
    parts = len(row_parts)
    rows, side = row_parts[0].shape
    vmem = pl.BlockSpec(memory_space=pltpu.VMEM)
    return pl.pallas_call(
        gram_kernel,
        in_specs=[pl.BlockSpec(memory_space=pltpu.SMEM)] + [vmem] * parts,
        out_specs=[vmem] * parts,
        out_shape=[jax.ShapeDtypeStruct((2 * side + side // 2, side), jnp.float32)] * parts,
        compiler_params=pltpu.CompilerParams(vmem_limit_bytes=16 * MIB),
        cost_estimate=pl.CostEstimate(
            flops=6 * parts * rows * side * side, bytes_accessed=2 * MIB, transcendentals=0
        ),
        name="gram_quarters",
    )(own, *row_parts)


def factor_block(matrix):
    side = matrix.shape[0]
    tiles = side // 8
    v = [matrix[8 * t : 8 * t + 8, :] for t in range(tiles)]
    lane = lax.broadcasted_iota(jnp.int32, (8, side), 1)
    sub = lax.broadcasted_iota(jnp.int32, (8, side), 0)
    inverse = []
    log_row = jnp.zeros((8, side), jnp.float32)
    for t0 in range(tiles):
        base = 8 * t0
        panel = v[t0]
        in_panel = (lane >= base) & (lane < base + 8)
        column = [jnp.broadcast_to(panel[:, base + q : base + q + 1], (8, side)) for q in range(8)]
        splat = [
            [jnp.broadcast_to(column[p][q : q + 1, :], (8, side)) for p in range(q + 1)]
            for q in range(8)
        ]
        recip, lower = [], [[None] * 8 for _ in range(8)]
        for p in range(8):
            recip.append(1.0 / splat[p][p])
            for q in range(p + 1, 8):
                lower[q][p] = splat[q][p] * recip[p]
            for q in range(p + 1, 8):
                for r in range(p + 1, q + 1):
                    splat[q][r] = splat[q][r] - lower[q][p] * splat[r][p]
        rows = []
        for q in range(8):
            own = jnp.broadcast_to(panel[q : q + 1, :], (8, side))
            own = jnp.where(in_panel, (lane == base + q).astype(jnp.float32), own)
            for p in range(q):
                own = own - lower[q][p] * rows[p]
            rows.append(own)
        for t in range(t0 + 1, tiles):
            reduced = []
            fresh = jnp.where(in_panel, 0.0, v[t])
            for p in range(8):
                mine = jnp.broadcast_to(v[t][:, base + p : base + p + 1], (8, side))
                for r in range(p):
                    mine = mine - lower[p][r] * reduced[r]
                reduced.append(mine)
                fresh = fresh - (mine * recip[p]) * rows[p]
            v[t] = fresh
        done, pivots = rows[0], splat[0][0]
        for q in range(1, 8):
            done = jnp.where(sub == q, rows[q], done)
            pivots = jnp.where(sub == q, splat[q][q], pivots)
        inverse.append(jnp.where(lane <= sub + base, done * lax.rsqrt(pivots), 0.0))
        log_row = log_row + jnp.where(lane == sub + base, 0.5 * jnp.log(pivots), 0.0)
    return jnp.concatenate(inverse, axis=0), jnp.sum(log_row, axis=0, keepdims=True)


def factor_kernel(scale, own_ref, *refs):
    inv_ref, log_ref, m_ref, z_ref = refs[-4:]
    parts = m_ref.shape[0]
    side = m_ref.shape[2]
    half = side // 2
    for a in range(parts):
        for b in range(a):
            m_ref[a, b] = jnp.zeros((side, side), jnp.float32)
    for k in range(parts):
        device = lax.rem(own_ref[0] + parts - k, parts)
        after = lax.rem(device + 1, parts)
        m_ref[device, device] = refs[k][:side, :] * scale
        second = refs[k][side : 2 * side, :] * scale
        m_ref[jnp.minimum(device, after), jnp.maximum(device, after)] = jnp.where(
            after < device, second.T, second
        )
        low = lax.rem(device, 2)
        m_ref[low, low + 2, pl.ds(pl.multiple_of(device // 2 * half, half), half), :] = (
            refs[k][2 * side :, :] * scale
        )
    sub = lax.broadcasted_iota(jnp.int32, (side, side), 0)
    lane = lax.broadcasted_iota(jnp.int32, (side, side), 1)
    eye = (sub == lane).astype(jnp.float32)

    @pl.loop(0, parts)
    def _(k):
        inverse, logs = factor_block(m_ref[k, k])
        log_ref[pl.ds(k, 1), :] = logs
        for b in range(parts):
            block = jnp.where(k == b, eye, m_ref[k, b])
            z_ref[b] = split_dot(inverse, block, 1, 0)
        for b in range(parts):
            inv_ref[k, b] = jnp.where(b <= k, z_ref[b], 0.0).astype(jnp.bfloat16)
        for a in range(1, parts):

            @pl.when(a > k)
            def _():
                for b in range(parts):
                    change = split_dot(z_ref[a], z_ref[b], 0, 0)
                    m_ref[a, b] = jnp.where(k == b, 0.0, m_ref[a, b]) - change


def cholesky_parts(own, quarters, unit_total):
    parts = len(quarters)
    side = quarters[0].shape[1]
    vmem = pl.BlockSpec(memory_space=pltpu.VMEM)
    return pl.pallas_call(
        functools.partial(factor_kernel, 1.0 / unit_total),
        in_specs=[pl.BlockSpec(memory_space=pltpu.SMEM)] + [vmem] * parts,
        out_specs=[vmem, vmem],
        out_shape=[
            jax.ShapeDtypeStruct((parts, parts, side, side), jnp.bfloat16),
            jax.ShapeDtypeStruct((parts, side), jnp.float32),
        ],
        scratch_shapes=[
            pltpu.VMEM((parts, parts, side, side), jnp.float32),
            pltpu.VMEM((parts, side, side), jnp.float32),
        ],
        compiler_params=pltpu.CompilerParams(vmem_limit_bytes=16 * MIB),
        cost_estimate=pl.CostEstimate(
            flops=200_000_000, bytes_accessed=2 * MIB, transcendentals=100_000
        ),
        name="factor",
    )(own, *quarters)


def renew_kernel(own_ref, *refs):
    s_refs, (inv_ref, out_ref) = refs[:-2], refs[-2:]
    own = own_ref[0]
    parts = len(s_refs)
    total = None
    for k in range(parts):
        term = lax.dot_general(
            s_refs[k][...],
            inv_ref[own, lax.rem(own + parts - k, parts)],
            (((1,), (1,)), ((), ())),
            preferred_element_type=jnp.float32,
        )
        total = term if total is None else total + term
    out_ref[...] = total.astype(jnp.bfloat16)


def renew(own, vectors, inverse):
    parts = len(vectors)
    rows, width = vectors[0].shape
    side = inverse.shape[-1]
    chunk = rows // 4
    rows_spec = pl.BlockSpec((chunk, width), lambda i, *_: (i, 0))
    return pl.pallas_call(
        renew_kernel,
        grid_spec=pltpu.PrefetchScalarGridSpec(
            num_scalar_prefetch=1,
            grid=(rows // chunk,),
            in_specs=[rows_spec] * parts
            + [pl.BlockSpec((parts, parts, side, side), lambda i, *_: (0, 0, 0, 0))],
            out_specs=pl.BlockSpec((chunk, side), lambda i, *_: (i, 0)),
        ),
        out_shape=jax.ShapeDtypeStruct((rows, side), jnp.bfloat16),
        compiler_params=pltpu.CompilerParams(vmem_limit_bytes=16 * MIB),
        cost_estimate=pl.CostEstimate(
            flops=2 * parts * rows * width * side, bytes_accessed=6 * MIB, transcendentals=0
        ),
        name="renew",
    )(own, *vectors, inverse)


def around(parts, step):
    return [(i, (i + step) % parts) for i in range(parts)]


def onward(parts, step):
    return [(i, i + step) for i in range(parts - step)]


def body(
    tangents,
    state,
    gain,
    local_w,
    local_row,
    local_col,
    remote_w,
    remote_row,
    remote_owner,
    remote_offset,
):
    rows_dev, width = tangents.shape
    side = local_w.shape[1]
    block_rows = rows_dev // side
    units = lax.axis_size("unit")
    parts = lax.axis_size("vec")
    unit_total = float(rows_dev * units)

    assert side == 2 * units and units <= 256 and block_rows <= 256
    blocks = tangents.reshape(block_rows, side, width)
    ask = jnp.concatenate([remote_owner[:, 0], remote_offset]).astype(jnp.bfloat16)
    far_count = remote_offset.shape[0]
    pieces, spread = spread_pieces(state, gain, blocks, ask.reshape(1, width), units)
    table = lax.all_to_all(spread, "unit", 0, 0, tiled=True)
    asked = table[:, 2 * block_rows, :].astype(jnp.float32)
    index = asked[:, :far_count] * block_rows + asked[:, far_count:]
    chosen = pick_rows(index, table, block_rows)
    arrived = lax.all_to_all(chosen, "unit", 0, 0, tiled=True)

    own = lax.axis_index("vec").astype(jnp.int32).reshape(1)
    steps = (2, 1, 3)
    assert parts == 4
    acc = local_product(local_row, local_col, local_w, pieces, blocks)
    stepped, *outgoing = far_product(own, remote_row, remote_w, acc, arrived, parts)

    row_parts = [outgoing[0]] + [None] * 3
    for k in steps:
        row_parts[k] = lax.ppermute(outgoing[k], "vec", around(parts, k))
    quarters = gram_quarters(own, [part.reshape(rows_dev // parts, width) for part in row_parts])
    mine = quarters[0]
    for k in steps:
        mine = mine + lax.ppermute(quarters[k], "vec", around(parts, k))

    late, mine = lax.optimization_barrier((stepped.reshape(rows_dev, width), mine))
    vectors = [late] + [None] * 3
    for k in steps:
        vectors[k] = lax.ppermute(late, "vec", onward(parts, k))

    share = mine.size // units
    by_unit = lax.all_to_all(mine.reshape(units, 1, share), "unit", 0, 0, tiled=True)
    summed = jnp.sum(by_unit, axis=0, keepdims=True)
    spread_sum = jnp.broadcast_to(summed, (units, 1, share))
    quarter = lax.all_to_all(spread_sum, "unit", 0, 0, tiled=True).reshape(mine.shape)
    gathered = [quarter] + [None] * 3
    for k in steps:
        gathered[k] = lax.ppermute(quarter, "vec", around(parts, k))

    inverse, logs = cholesky_parts(own, gathered, unit_total)
    renewed = renew(own, vectors, inverse)
    return (renewed, logs.reshape(parts * width))


def solution(mesh):
    placed = (
        P("unit", "vec"),
        P("unit"),
        P("unit"),
        P("unit", None, None),
        P("unit"),
        P("unit"),
        P("unit", None, None),
        P("unit"),
        P("unit", None),
        P("unit"),
    )
    return jax.shard_map(
        body, mesh=mesh, in_specs=placed, out_specs=(P("unit", "vec"), P()), check_vma=False
    )
```

time: 638 us -> 237 us (0.37)
  other arithmetic: 200 us -> 1.67 us
  waiting for transfers between devices: 268 us -> 71 us
  blocking collectives: 18.1 us -> 77.8 us
  local copies, waits for them, and re-layouts: 69.7 us -> 13.3 us
  Pallas kernels: 0 us -> 44.3 us
  matrix products: 35.4 us -> 0 us
  between operations: 17.1 us -> 0.79 us
    psum x1 -> x0, waiting for transfers between devices: 250 us -> none  [body(): gram_matrix = lax.psum(partial_gram, ('unit', 'vec')) / unit_total]
    another operation x17 -> x0, other arithmetic: 121 us -> none  [the longest x14 78.9 us: cholesky_parts(): lower_factor = jnp.linalg.cholesky(gram_matrix)]
    scatter-add x2 -> x0, other arithmetic: 64.7 us -> none  [the longest x1 51.3 us: body(): jax.ops.segment_sum(local_terms, local_row, num_segments=block_rows)]
    all_to_all x1 -> x3, blocking collectives: 18.1 us -> 77.8 us  [the longest x1 44.3 us: body(): table = lax.all_to_all(spread, 'unit', 0, 0, tiled=True)]
    pallas_call x0 -> x7, Pallas kernels: none -> 44.3 us  [the longest x1 22.4 us: cholesky_parts(): pl.pallas_call(functools.partial(factor_kernel, 1.0 / unit_total), in_spe...]
    ppermute x0 -> x12, waiting for transfers between devices: none -> 34 us  [the longest x3 17.7 us: body(): gathered[k] = lax.ppermute(quarter, 'vec', around(parts, k))]
    dot_general x2 -> x0, local copies, waits for them, and re-layouts: 23.1 us -> none  [the longest x1 17.5 us: body(): jnp.einsum('bij,bjk->bik', local_w, near_blocks, preferred_element_type=j...]
    dot_general x4 -> x0, matrix products: 23 us -> none  [the longest x1 12.8 us: body(): jnp.einsum('bij,bjk->bik', local_w, near_blocks, preferred_element_type=j...]
  transfers between devices with their start and end apart: 4 -> 13, of which waited for: 4 -> 8; matrix products, arithmetic and copies ran while one was open for 16% -> 0% of each run, Pallas kernels for 0% -> 13%
where the time goes in v1:
time: 237 us; the launch traced here: 235 us
  blocking collectives  77.8 us (33%)
  waiting for transfers between devices  71 us (30%)
  Pallas kernels  44.3 us (19%)
  starting transfers between devices  25.8 us (11%)
  local copies, waits for them, and re-layouts  13.3 us (6%)
    all_to_all x1, blocking collectives, body(): table = lax.all_to_all(spread, 'unit', 0, 0, tiled=True)  44.3 us
    all_to_all x1, waiting for transfers between devices, body(): arrived = lax.all_to_all(chosen, 'unit', 0, 0, tiled=True)  37 us
    pallas_call x1, Pallas kernels, cholesky_parts(): pl.pallas_call(functools.partial(factor_kernel, 1.0 / unit_total), in_spe...  22.4 us
    ppermute x3, waiting for transfers between devices, body(): gathered[k] = lax.ppermute(quarter, 'vec', around(parts, k))  17.7 us
    all_to_all x1, blocking collectives, body(): lax.all_to_all(mine.reshape(units, 1, share), 'unit', 0, 0, tiled=True)  17.7 us
    all_to_all x1, blocking collectives, body(): lax.all_to_all(spread_sum, 'unit', 0, 0, tiled=True).reshape(mine.shape)  15.7 us
    unnamed x28, local copies, waits for them, and re-layouts  13.1 us
    ppermute x3, waiting for transfers between devices, body(): row_parts[k] = lax.ppermute(outgoing[k], 'vec', around(parts, k))  10.5 us
  transfers between devices with their start and end apart: 13, of which 8 were waited for; matrix products, arithmetic and copies ran while one was open for 0% of the time, Pallas kernels for 13%

profile of v1, /device:TPU:1, one launch (start us, length us, event | category | flops | bytes accessed | tf_op | source)
XLA Modules:
  0.0 234.6 jit_solution(6809926604755928989)
XLA Ops:
  2.0 1.2 copy-done.3
  5.5 44.3 %all_to_all.20.table_ref = bf16[64,72,128]{2,1,0:T(8,128)(2,1)S(1)} all-to-all(bf16[64,72,128]{2,1,0:T(8,128)(2,1)S(1)} %get-tuple-element.18), channel_id=1, replica_groups=mesh['unit'=64,'vec'=4] {'unit'}, dimensions={0} | all-to-all | bytes 2359296 | tf_op jit(solution)/shard_map/all_to_all | solution.py:429
  50.0 5.2 %pick_rows.1 = bf16[64,128,128]{2,1,0:T(8,128)(2,1)S(1)} custom-call(f32[4,8,128]{2,1,0:T(8,128)S(1)} %reshape.87.index_ref, bf16[64,72,128]{2,1,0:T(8,128)(2,1)S(1)} %all_to_all.20.table_ref), custom_call_target="tpu_custom_call" | custom-call | flops 4000000000 | bytes 4194304 | tf_op jit(solution)/shard_map/pick_rows/pallas_call | solution.py:141
  55.3 1.3 copy-done.6
  56.6 6.3 %all-to-all-start.1 = ((bf16[64,128,128]{2,1,0:T(8,128)(2,1)}), bf16[64,128,128]{2,1,0:T(8,128)(2,1)S(1)}, u32[]{:S(2)}, u32[]{:S(2)}) async-start(bf16[64,128,128]{2,1,0:T(8,128)(2,1)} %copy-done.6), calls=%async_computation.1 | async-start | bytes 4194304 | tf_op jit(solution)/shard_map/all_to_all | solution.py:433
  63.0 3.4 %copy-done = bf16[256,128,128]{2,1,0:T(8,128)(2,1)S(1)} copy-done((bf16[256,128,128]{2,1,0:T(8,128)(2,1)S(1)}, bf16[256,128,128]{2,1,0:T(8,128)(2,1)}, u32[]{:S(2)}) %copy-start) | copy-done | bytes 8388632
  66.4 1.2 copy-done.8
  67.6 8.3 %local_blocks.1.acc_in_ref = f32[32,128,128]{2,1,0:T(8,128)S(1)} custom-call(s32[256]{0:T(256)S(1)} %copy-done.11, s32[256]{0:T(256)S(1)} %copy-done.12, bf16[256,128,128]{2,1,0:T(8,128)(2,1)S(1)} %copy-done, bf16[32,128,128]{2,1,0:T(8,128)(2,1)S(1)} %copy-done.8, bf16[32,128,128]{2,1,0:T(8,128)(2,1)S(1)} %bitcast.18), custom_call_target="tpu_custom_call" | custom-call | flops 1073741824 | bytes 14680064 | tf_op jit(solution)/shard_map/local_blocks/pallas_call | solution.py:47
  75.9 1.3 copy-done.1
  77.2 37.0 %all-to-all-done.1.arrived_ref = bf16[64,128,128]{2,1,0:T(8,128)(2,1)S(1)} async-done(((bf16[64,128,128]{2,1,0:T(8,128)(2,1)}), bf16[64,128,128]{2,1,0:T(8,128)(2,1)S(1)}, u32[]{:S(2)}, u32[]{:S(2)}) %all-to-all-start.1) | async-done | bytes 2097184 | tf_op jit(solution)/shard_map/all_to_all | solution.py:433
  114.2 1.6 copy-done.2
  115.8 1.6 copy-done.5
  117.4 2.5 %far_blocks.1 = (bf16[32,128,128]{2,1,0:T(8,128)(2,1)S(1)}, bf16[8,128,128]{2,1,0:T(8,128)(2,1)S(1)}, bf16[8,128,128]{2,1,0:T(8,128)(2,1)S(1)}, bf16[8,128,128]{2,1,0:T(8,128)(2,1)S(1)}, bf16[8,128,128]{2,1,0:T(8,128)(2,1)S(1)}) custom-call(s32[1]{0:T(128)} %bitcast.own_ref, s32[64]{0:T(128)S(1)} %copy-done.13, bf16[64,128,128]{2,1,0:T(8,128)(2,1)S(1)} %copy-done.5, ...), custom_call_target="tpu_custom_call" | custom-call | flops 268435456 | bytes 8388608 | tf_op jit(solution)/shard_map/far_blocks/pallas_call | solution.py:184
  119.9 1.3 collective-permute-start
  121.2 2.4 %collective-permute-start.1 = (bf16[8,128,128]{2,1,0:T(8,128)(2,1)S(1)}, bf16[8,128,128]{2,1,0:T(8,128)(2,1)S(1)}, u32[]{:S(2)}, u32[]{:S(2)}) collective-permute-start(bf16[8,128,128]{2,1,0:T(8,128)(2,1)S(1)} %get-tuple-element.22), channel_id=1, source_target_pairs={{0,2},{1,3},{2,0},{3,1},{4,6},{5,7},{6,4},{7,5},{8,10},{9,11},{10,... | collective-permute-start | bytes 786440 | tf_op jit(solution)/shard_map/ppermute | solution.py:443
  123.7 1.2 collective-permute-start.2
  124.8 3.9 %collective-permute-done = bf16[8,128,128]{2,1,0:T(8,128)(2,1)S(1)} collective-permute-done((bf16[8,128,128]{2,1,0:T(8,128)(2,1)S(1)}, bf16[8,128,128]{2,1,0:T(8,128)(2,1)S(1)}, u32[]{:S(2)}, u32[]{:S(2)}) %collective-permute-start) | collective-permute-done | bytes 262176 | tf_op jit(solution)/shard_map/ppermute | solution.py:443
  128.7 6.6 %collective-permute-done.1 = bf16[8,128,128]{2,1,0:T(8,128)(2,1)S(1)} collective-permute-done((bf16[8,128,128]{2,1,0:T(8,128)(2,1)S(1)}, bf16[8,128,128]{2,1,0:T(8,128)(2,1)S(1)}, u32[]{:S(2)}, u32[]{:S(2)}) %collective-permute-start.1) | collective-permute-done | bytes 262176 | tf_op jit(solution)/shard_map/ppermute | solution.py:443
  136.1 2.2 collective-permute-start.3
  138.3 1.2 collective-permute-start.4
  139.5 1.5 collective-permute-start.5
  141.0 0.9 collective-permute-done.3
  141.9 4.4 %collective-permute-done.4 = f32[320,128]{1,0:T(8,128)S(1)} collective-permute-done((f32[320,128]{1,0:T(8,128)S(1)}, f32[320,128]{1,0:T(8,128)S(1)}, u32[]{:S(2)}, u32[]{:S(2)}) %collective-permute-start.4) | collective-permute-done | bytes 163872 | tf_op jit(solution)/shard_map/ppermute | solution.py:447
  146.9 4.4 %collective-permute-start.8 = (bf16[4096,128]{1,0:T(8,128)(2,1)S(1)}, bf16[4096,128]{1,0:T(8,128)(2,1)S(1)}, u32[]{:S(2)}, u32[]{:S(2)}) collective-permute-start(bf16[4096,128]{1,0:T(8,128)(2,1)S(1)} %bitcast.19), channel_id=1, source_target_pairs={{0,3},{4,7},{8,11},{12,15},{16,19},{20,23},{24,27},{28,31},{32,35}... | collective-permute-start | bytes 3145736 | tf_op jit(solution)/shard_map/ppermute | solution.py:452
  151.3 1.4 collective-permute-start.7
  152.6 3.4 %collective-permute-start.6 = (bf16[4096,128]{1,0:T(8,128)(2,1)S(1)}, bf16[4096,128]{1,0:T(8,128)(2,1)}, u32[]{:S(2)}, u32[]{:S(2)}) collective-permute-start(bf16[4096,128]{1,0:T(8,128)(2,1)S(1)} %bitcast.21), channel_id=1, source_target_pairs={{0,1},{1,2},{2,3},{4,5},{5,6},{6,7},{8,9},{9,10},{10,11},{12,13},{... | collective-permute-start | bytes 3145736 | tf_op jit(solution)/shard_map/ppermute | solution.py:452
  156.1 17.7 %all_to_all.21 = f32[64,1,640]{2,1,0:T(1,128)S(1)} all-to-all(f32[64,1,640]{2,1,0:T(1,128)S(1)} %bitcast.33), channel_id=1, replica_groups=mesh['unit'=64,'vec'=4] {'unit'}, dimensions={0} | all-to-all | bytes 327680 | tf_op jit(solution)/shard_map/all_to_all | solution.py:455
  174.0 15.7 %all_to_all.22 = f32[64,1,640]{2,1,0:T(1,128)S(1)} all-to-all(f32[64,1,640]{2,1,0:T(1,128)S(1)} %broadcast_in_dim.2), channel_id=1, replica_groups=mesh['unit'=64,'vec'=4] {'unit'}, dimensions={0} | all-to-all | bytes 327680 | tf_op jit(solution)/shard_map/all_to_all | solution.py:458
  190.3 11.6 %collective-permute-done.11.refs_3_ = f32[320,128]{1,0:T(8,128)S(1)} collective-permute-done((f32[320,128]{1,0:T(8,128)S(1)}, f32[320,128]{1,0:T(8,128)S(1)}, u32[]{:S(2)}, u32[]{:S(2)}) %collective-permute-start.11) | collective-permute-done | bytes 163872 | tf_op jit(solution)/shard_map/ppermute | solution.py:461
  201.9 6.1 %collective-permute-done.9.refs_1_ = f32[320,128]{1,0:T(8,128)S(1)} collective-permute-done((f32[320,128]{1,0:T(8,128)S(1)}, f32[320,128]{1,0:T(8,128)S(1)}, u32[]{:S(2)}, u32[]{:S(2)}) %collective-permute-start.9) | collective-permute-done | bytes 163872 | tf_op jit(solution)/shard_map/ppermute | solution.py:461
  208.0 22.4 %factor.1 = (bf16[4,4,128,128]{3,2,1,0:T(8,128)(2,1)S(1)}, f32[4,128]{1,0:T(4,128)}) custom-call(s32[1]{0:T(128)} %bitcast.own_ref, f32[320,128]{1,0:T(8,128)S(1)} %bitcast.26, f32[320,128]{1,0:T(8,128)S(1)} %collective-permute-done.9.refs_1_, f32[320,128]{1,0:T(8,128)S(1)} %collective-permute-done.10.refs_2_, f32[320,128]{1,0:T(8,128)S(1)} %collective-permute-done.11.refs_3_), custom_call_target="tpu_custom_call" | custom-call | flops 200000000 | bytes 2097152 | tf_op jit(solution)/shard_map/factor/pallas_call | solution.py:337
  230.4 4.2 %renew.1 = bf16[4096,128]{1,0:T(8,128)(2,1)} custom-call(s32[1]{0:T(128)} %bitcast.own_ref, bf16[4096,128]{1,0:T(8,128)(2,1)S(1)} %bitcast.22, bf16[4096,128]{1,0:T(8,128)(2,1)} %collective-permute-done.6.refs_1_, bf16[4096,128]{1,0:T(8,128)(2,1)S(1)} %collective-permute-done.7.refs_2_, bf16[4096,128]{1,0:T(8,128)(2,1)S(1)} %collective-permute-done.8.refs_3_, ...), custom_call_target="tpu_custom_call" | custom-call | flops 536870912 | bytes 6291456 | tf_op jit(solution)/shard_map/renew/pallas_call | solution.py:379
  (41 shorter events, 6.0 us)
Async XLA Ops:
  2.0 1.2 copy-start.3
  3.3 0.7 copy-start.9
  4.0 0.7 copy-start.10
  5.5 44.3 %copy-start.7 = (bf16[32,128,128]{2,1,0:T(8,128)(2,1)}, bf16[32,128,128]{2,1,0:T(8,128)(2,1)S(1)}, u32[]{:S(2)}) copy-start(bf16[32,128,128]{2,1,0:T(8,128)(2,1)S(1)} %get-tuple-element.17.x_ref) | copy-start | bytes 3145732
  55.3 1.3 copy-start.6
  56.6 6.3 %copy-start.4 = (bf16[4096,128]{1,0:T(8,128)(2,1)S(1)}, bf16[4096,128]{1,0:T(8,128)(2,1)}, u32[]{:S(2)}) copy-start(bf16[4096,128]{1,0:T(8,128)(2,1)} %param.10) | copy-start | bytes 3145732
  56.6 6.3 %copy-start.11 = (s32[256]{0:T(256)S(1)}, s32[256]{0:T(256)}, u32[]{:S(2)}) copy-start(s32[256]{0:T(256)} %row_ref.2) | copy-start | bytes 3076
  56.6 6.4 %copy-start.12 = (s32[256]{0:T(256)S(1)}, s32[256]{0:T(256)}, u32[]{:S(2)}) copy-start(s32[256]{0:T(256)} %col_ref.1) | copy-start | bytes 3076
  56.6 57.6 %all-to-all-start.1 = ((bf16[64,128,128]{2,1,0:T(8,128)(2,1)}), bf16[64,128,128]{2,1,0:T(8,128)(2,1)S(1)}, u32[]{:S(2)}, u32[]{:S(2)}) async-start(bf16[64,128,128]{2,1,0:T(8,128)(2,1)} %copy-done.6), calls=%async_computation.1 | async-start | bytes 4194304 | tf_op jit(solution)/shard_map/all_to_all | solution.py:433
  63.0 3.4 %copy-start = (bf16[256,128,128]{2,1,0:T(8,128)(2,1)S(1)}, bf16[256,128,128]{2,1,0:T(8,128)(2,1)}, u32[]{:S(2)}) copy-start(bf16[256,128,128]{2,1,0:T(8,128)(2,1)} %w_ref.2) | copy-start | bytes 25165828
  66.4 1.2 copy-start.8
  67.6 46.6 %copy-start.13 = (s32[64]{0:T(128)S(1)}, s32[64]{0:T(128)}, u32[]{:S(2)}) copy-start(s32[64]{0:T(128)} %row_ref.3) | copy-start | bytes 772
  75.9 1.3 copy-start.1
  114.2 1.6 copy-start.2
  115.8 1.6 copy-start.5
  119.9 8.8 %collective-permute-start = (bf16[8,128,128]{2,1,0:T(8,128)(2,1)S(1)}, bf16[8,128,128]{2,1,0:T(8,128)(2,1)S(1)}, u32[]{:S(2)}, u32[]{:S(2)}) collective-permute-start(bf16[8,128,128]{2,1,0:T(8,128)(2,1)S(1)} %get-tuple-element.21), channel_id=1, source_target_pairs={{0,1},{1,2},{2,3},{3,0},{4,5},{5,6},{6,7},{7,4},{8,9},{9,10},{10,1... | collective-permute-start | bytes 786440 | tf_op jit(solution)/shard_map/ppermute | solution.py:443
  121.2 14.1 %collective-permute-start.1 = (bf16[8,128,128]{2,1,0:T(8,128)(2,1)S(1)}, bf16[8,128,128]{2,1,0:T(8,128)(2,1)S(1)}, u32[]{:S(2)}, u32[]{:S(2)}) collective-permute-start(bf16[8,128,128]{2,1,0:T(8,128)(2,1)S(1)} %get-tuple-element.22), channel_id=1, source_target_pairs={{0,2},{1,3},{2,0},{3,1},{4,6},{5,7},{6,4},{7,5},{8,10},{9,11},{10,... | collective-permute-start | bytes 786440 | tf_op jit(solution)/shard_map/ppermute | solution.py:443
  123.7 11.6 %collective-permute-start.2 = (bf16[8,128,128]{2,1,0:T(8,128)(2,1)S(1)}, bf16[8,128,128]{2,1,0:T(8,128)(2,1)S(1)}, u32[]{:S(2)}, u32[]{:S(2)}) collective-permute-start(bf16[8,128,128]{2,1,0:T(8,128)(2,1)S(1)} %get-tuple-element.23), channel_id=1, source_target_pairs={{0,3},{1,0},{2,1},{3,2},{4,7},{5,4},{6,5},{7,6},{8,11},{9,8},{10,9... | collective-permute-start | bytes 786440 | tf_op jit(solution)/shard_map/ppermute | solution.py:443
  136.1 5.8 %collective-permute-start.3 = (f32[320,128]{1,0:T(8,128)S(1)}, f32[320,128]{1,0:T(8,128)S(1)}, u32[]{:S(2)}, u32[]{:S(2)}) collective-permute-start(f32[320,128]{1,0:T(8,128)S(1)} %get-tuple-element.25), channel_id=1, source_target_pairs={{0,2},{1,3},{2,0},{3,1},{4,6},{5,7},{6,4},{7,5},{8,10},{9,11},{10,... | collective-permute-start | bytes 491528 | tf_op jit(solution)/shard_map/ppermute | solution.py:447
  138.3 8.0 %collective-permute-start.4 = (f32[320,128]{1,0:T(8,128)S(1)}, f32[320,128]{1,0:T(8,128)S(1)}, u32[]{:S(2)}, u32[]{:S(2)}) collective-permute-start(f32[320,128]{1,0:T(8,128)S(1)} %get-tuple-element.26), channel_id=1, source_target_pairs={{0,1},{1,2},{2,3},{3,0},{4,5},{5,6},{6,7},{7,4},{8,9},{9,10},{10,1... | collective-permute-start | bytes 491528 | tf_op jit(solution)/shard_map/ppermute | solution.py:447
  139.5 7.3 %collective-permute-start.5 = (f32[320,128]{1,0:T(8,128)S(1)}, f32[320,128]{1,0:T(8,128)S(1)}, u32[]{:S(2)}, u32[]{:S(2)}) collective-permute-start(f32[320,128]{1,0:T(8,128)S(1)} %get-tuple-element.27), channel_id=1, source_target_pairs={{0,3},{1,0},{2,1},{3,2},{4,7},{5,4},{6,5},{7,6},{8,11},{9,8},{10,9... | collective-permute-start | bytes 491528 | tf_op jit(solution)/shard_map/ppermute | solution.py:447
  146.9 83.5 %collective-permute-start.8 = (bf16[4096,128]{1,0:T(8,128)(2,1)S(1)}, bf16[4096,128]{1,0:T(8,128)(2,1)S(1)}, u32[]{:S(2)}, u32[]{:S(2)}) collective-permute-start(bf16[4096,128]{1,0:T(8,128)(2,1)S(1)} %bitcast.19), channel_id=1, source_target_pairs={{0,3},{4,7},{8,11},{12,15},{16,19},{20,23},{24,27},{28,31},{32,35}... | collective-permute-start | bytes 3145736 | tf_op jit(solution)/shard_map/ppermute | solution.py:452
  151.3 79.1 %collective-permute-start.7 = (bf16[4096,128]{1,0:T(8,128)(2,1)S(1)}, bf16[4096,128]{1,0:T(8,128)(2,1)S(1)}, u32[]{:S(2)}, u32[]{:S(2)}) collective-permute-start(bf16[4096,128]{1,0:T(8,128)(2,1)S(1)} %bitcast.20), channel_id=1, source_target_pairs={{0,2},{1,3},{4,6},{5,7},{8,10},{9,11},{12,14},{13,15},{16,18},{17,... | collective-permute-start | bytes 3145736 | tf_op jit(solution)/shard_map/ppermute | solution.py:452
  152.6 77.8 %collective-permute-start.6 = (bf16[4096,128]{1,0:T(8,128)(2,1)S(1)}, bf16[4096,128]{1,0:T(8,128)(2,1)}, u32[]{:S(2)}, u32[]{:S(2)}) collective-permute-start(bf16[4096,128]{1,0:T(8,128)(2,1)S(1)} %bitcast.21), channel_id=1, source_target_pairs={{0,1},{1,2},{2,3},{4,5},{5,6},{6,7},{8,9},{9,10},{10,11},{12,13},{... | collective-permute-start | bytes 3145736 | tf_op jit(solution)/shard_map/ppermute | solution.py:452
  189.7 12.2 %collective-permute-start.11 = (f32[320,128]{1,0:T(8,128)S(1)}, f32[320,128]{1,0:T(8,128)S(1)}, u32[]{:S(2)}, u32[]{:S(2)}) collective-permute-start(f32[320,128]{1,0:T(8,128)S(1)} %bitcast.23), channel_id=1, source_target_pairs={{0,3},{1,0},{2,1},{3,2},{4,7},{5,4},{6,5},{7,6},{8,11},{9,8},{10,9... | collective-permute-start | bytes 491528 | tf_op jit(solution)/shard_map/ppermute | solution.py:461
  189.7 12.2 %collective-permute-start.10 = (f32[320,128]{1,0:T(8,128)S(1)}, f32[320,128]{1,0:T(8,128)S(1)}, u32[]{:S(2)}, u32[]{:S(2)}) collective-permute-start(f32[320,128]{1,0:T(8,128)S(1)} %bitcast.24), channel_id=1, source_target_pairs={{0,2},{1,3},{2,0},{3,1},{4,6},{5,7},{6,4},{7,5},{8,10},{9,11},{10,... | collective-permute-start | bytes 491528 | tf_op jit(solution)/shard_map/ppermute | solution.py:461
  201.9 6.1 %collective-permute-start.9 = (f32[320,128]{1,0:T(8,128)S(1)}, f32[320,128]{1,0:T(8,128)S(1)}, u32[]{:S(2)}, u32[]{:S(2)}) collective-permute-start(f32[320,128]{1,0:T(8,128)S(1)} %bitcast.25), channel_id=1, source_target_pairs={{0,1},{1,2},{2,3},{3,0},{4,5},{5,6},{6,7},{7,4},{8,9},{9,10},{10,1... | collective-permute-start | bytes 491528 | tf_op jit(solution)/shard_map/ppermute | solution.py:461

commit v2 on v1

--- a/solution.py
+++ b/solution.py
@@ -56,7 +56,7 @@
             ],
             out_specs=pl.BlockSpec((block_rows, side, width), whole),
         ),
-        out_shape=jax.ShapeDtypeStruct((block_rows, side, width), jnp.float32),
+        out_shape=pltpu.HBM((block_rows, side, width), jnp.float32),
         compiler_params=pltpu.CompilerParams(vmem_limit_bytes=16 * MIB),
         cost_estimate=pl.CostEstimate(
             flops=2 * count * side * side * width, bytes_accessed=14 * MIB, transcendentals=0
@@ -69,11 +69,30 @@
     return jnp.broadcast_to(row, (side, side)).T
 
 
-def spread_kernel(state_ref, gain_ref, t_ref, ask_ref, pieces_ref, spread_ref):
+def spread_kernel(*refs):
+    sources, (pieces_ref, spread_ref), targets, sems = refs[:5], refs[5:7], refs[7:12], refs[12]
+    owner_ref, offset_ref, state_ref, gain_ref, t_ref = targets
+    copies = [
+        pltpu.make_async_copy(source, target, sems.at[i])
+        for i, (source, target) in enumerate(zip(sources, targets))
+    ]
+    for copy in copies:
+        copy.start()
     block_rows, side, width = t_ref.shape
     half = side // 2
+    units, rows, _ = spread_ref.shape
+    extra = rows - 2 * block_rows
+    copies[0].wait()
+    copies[1].wait()
+    ask = jnp.concatenate([owner_ref[...], offset_ref[...]], axis=1).astype(jnp.float32)
+    spread_ref[:, 2 * block_rows :, :] = jnp.broadcast_to(
+        ask.reshape(1, 1, width), (units, extra, width)
+    ).astype(jnp.bfloat16)
+    copies[2].wait()
+    copies[3].wait()
     gain = gain_ref[...]
     slopes = gain * (1.0 - jnp.tanh(gain * state_ref[...]) ** 2)
+    copies[4].wait()
     for p in range(block_rows):
         slope = column_of(slopes[p : p + 1, :], side)
         pieces_ref[p] = (slope * t_ref[p].astype(jnp.float32)).astype(jnp.bfloat16)
@@ -82,31 +101,48 @@
             group = pieces_ref[16 * g : 16 * g + 16, h * half : (h + 1) * half, :]
             at = h * block_rows + 16 * g
             spread_ref[:, at : at + 16, :] = jnp.swapaxes(group, 0, 1)
-    units, rows, _ = spread_ref.shape
-    extra = rows - 2 * block_rows
-    spread_ref[:, 2 * block_rows :, :] = jnp.broadcast_to(
-        ask_ref[...].reshape(1, 1, width), (units, extra, width)
-    )
-
-
-def spread_pieces(state, gain, blocks, ask, units):
+
+
+def in_hbm(*arrays):
+    return [pltpu.with_memory_space_constraint(array, pltpu.HBM) for array in arrays]
+
+
+def spread_pieces(state, gain, blocks, owner, offset, units):
     block_rows, side, width = blocks.shape
     rows = 2 * block_rows + 8
+    count = offset.shape[0]
     vmem = pl.BlockSpec(memory_space=pltpu.VMEM)
+    hbm = pl.BlockSpec(memory_space=pltpu.HBM)
     return pl.pallas_call(
         spread_kernel,
-        in_specs=[vmem] * 4,
+        in_specs=[hbm] * 5,
         out_specs=[vmem] * 2,
         out_shape=[
             jax.ShapeDtypeStruct((block_rows, side, width), jnp.bfloat16),
             jax.ShapeDtypeStruct((units, rows, width), jnp.bfloat16),
         ],
+        scratch_shapes=[
+            pltpu.VMEM((1, count), jnp.int32),
+            pltpu.VMEM((1, count), jnp.int32),
+            pltpu.VMEM((block_rows, side), jnp.float32),
+            pltpu.VMEM((block_rows, side), jnp.float32),
+            pltpu.VMEM((block_rows, side, width), jnp.bfloat16),
+            pltpu.SemaphoreType.DMA((5,)),
+        ],
         compiler_params=pltpu.CompilerParams(vmem_limit_bytes=16 * MIB),
         cost_estimate=pl.CostEstimate(
             flops=4 * MIB, bytes_accessed=4 * MIB, transcendentals=block_rows * side
         ),
         name="spread_pieces",
-    )(state.reshape(block_rows, side), gain.reshape(block_rows, side), blocks, ask)
+    )(
+        *in_hbm(
+            owner.reshape(1, count),
+            offset.reshape(1, count),
+            state.reshape(block_rows, side),
+            gain.reshape(block_rows, side),
+            blocks,
+        )
+    )
 
 
 def pick_kernel(block_rows, index_ref, table_ref, out_ref):
@@ -146,7 +182,7 @@
             pl.BlockSpec(table.shape, lambda i: (0, 0, 0)),
         ],
         out_specs=pl.BlockSpec((units // steps, 2 * far_count, width), lambda i: (i, 0, 0)),
-        out_shape=jax.ShapeDtypeStruct((units, 2 * far_count, width), jnp.bfloat16),
+        out_shape=pltpu.HBM((units, 2 * far_count, width), jnp.bfloat16),
         compiler_params=pltpu.CompilerParams(vmem_limit_bytes=32 * MIB),
         cost_estimate=pl.CostEstimate(
             flops=4_000_000_000, bytes_accessed=4 * MIB, transcendentals=0
@@ -155,48 +191,66 @@
     )(index.reshape(steps, lines, width), table)
 
 
-def far_kernel(own_ref, row_ref, w_ref, acc_in_ref, arrived_ref, out_ref, *rest):
-    part_refs, (acc_ref, x_ref) = rest[:-2], rest[-2:]
+def far_kernel(own_ref, row_ref, w_hbm, acc_hbm, arrived_ref, *rest):
+    part_refs, (far_ref, acc_ref, w_ref, x_ref, sems) = rest[:-5], rest[-5:]
     count = w_ref.shape[0]
     units = arrived_ref.shape[0]
-    acc_ref[...] = acc_in_ref[...]
-    for g in range(count // 16):
+    groups = count // 16
+    w_copies = [
+        pltpu.make_async_copy(
+            w_hbm.at[pl.ds(16 * g, 16)], w_ref.at[pl.ds(16 * g, 16)], sems.at[g]
+        )
+        for g in range(groups)
+    ]
+    acc_copy = pltpu.make_async_copy(acc_hbm, acc_ref, sems.at[groups])
+    for copy in w_copies:
+        copy.start()
+    acc_copy.start()
+    far_ref[...] = jnp.zeros_like(far_ref)
+    for g in range(groups):
         for h in range(2):
             at = h * count + 16 * g
             x_ref[16 * g : 16 * g + 16, h * units : (h + 1) * units, :] = jnp.swapaxes(
                 arrived_ref[:, at : at + 16, :], 0, 1
             )
+    for g in range(groups):
+        w_copies[g].wait()
         for inner in range(16):
             block = 16 * g + inner
             row = row_ref[block]
-            acc_ref[row] += jnp.dot(w_ref[block], x_ref[block], preferred_element_type=jnp.float32)
-    out_ref[...] = (time_step * acc_ref[...]).astype(jnp.bfloat16)
+            far_ref[row] += jnp.dot(w_ref[block], x_ref[block], preferred_element_type=jnp.float32)
+    acc_copy.wait()
     parts = len(part_refs)
     for k in range(parts):
         share = part_refs[k].shape[0]
-        part_refs[k][...] = out_ref[pl.ds(lax.rem(own_ref[0] + k, parts) * share, share)]
+        here = pl.ds(lax.rem(own_ref[0] + k, parts) * share, share)
+        part_refs[k][...] = (time_step * (acc_ref[here] + far_ref[here])).astype(jnp.bfloat16)
 
 
 def far_product(own, remote_row, remote_w, acc, arrived, parts):
     count, side, _ = remote_w.shape
     block_rows, _, width = acc.shape
     vmem = pl.BlockSpec(memory_space=pltpu.VMEM)
+    smem = pl.BlockSpec(memory_space=pltpu.SMEM)
+    hbm = pl.BlockSpec(memory_space=pltpu.HBM)
     return pl.pallas_call(
         far_kernel,
-        in_specs=[pl.BlockSpec(memory_space=pltpu.SMEM)] * 2 + [vmem] * 3,
-        out_specs=[vmem] * (1 + parts),
-        out_shape=[jax.ShapeDtypeStruct((block_rows, side, width), jnp.bfloat16)]
-        + [jax.ShapeDtypeStruct((block_rows // parts, side, width), jnp.bfloat16)] * parts,
+        in_specs=[smem, smem, hbm, hbm, vmem],
+        out_specs=[vmem] * parts,
+        out_shape=[jax.ShapeDtypeStruct((block_rows // parts, side, width), jnp.bfloat16)] * parts,
         scratch_shapes=[
             pltpu.VMEM((block_rows, side, width), jnp.float32),
+            pltpu.VMEM((block_rows, side, width), jnp.float32),
+            pltpu.VMEM((count, side, side), jnp.bfloat16),
             pltpu.VMEM((count, side, width), jnp.bfloat16),
-        ],
-        compiler_params=pltpu.CompilerParams(vmem_limit_bytes=20 * MIB),
+            pltpu.SemaphoreType.DMA((count // 16 + 1,)),
+        ],
+        compiler_params=pltpu.CompilerParams(vmem_limit_bytes=24 * MIB),
         cost_estimate=pl.CostEstimate(
             flops=2 * count * side * side * width, bytes_accessed=8 * MIB, transcendentals=0
         ),
         name="far_blocks",
-    )(own, remote_row, remote_w, acc, arrived)
+    )(own, remote_row, *in_hbm(remote_w, acc), arrived)
 
 
 def cross(left, right):
@@ -355,51 +409,44 @@
 
 
 def renew_kernel(own_ref, *refs):
-    s_refs, (inv_ref, out_ref) = refs[:-2], refs[-2:]
+    x_refs, (inv_ref, out_ref) = refs[:-2], refs[-2:]
     own = own_ref[0]
-    parts = len(s_refs)
-    total = None
-    for k in range(parts):
-        term = lax.dot_general(
-            s_refs[k][...],
-            inv_ref[own, lax.rem(own + parts - k, parts)],
-            (((1,), (1,)), ((), ())),
-            preferred_element_type=jnp.float32,
-        )
-        total = term if total is None else total + term
-    out_ref[...] = total.astype(jnp.bfloat16)
-
-
-def renew(own, vectors, inverse):
-    parts = len(vectors)
-    rows, width = vectors[0].shape
+    parts = len(x_refs)
+    for b in range(parts):
+        total = None
+        for k in range(parts):
+            term = lax.dot_general(
+                x_refs[k][...],
+                inv_ref[b, lax.rem(own + parts - k, parts)],
+                (((1,), (1,)), ((), ())),
+                preferred_element_type=jnp.float32,
+            )
+            total = term if total is None else total + term
+        out_ref[b] = total.astype(jnp.bfloat16)
+
+
+def renew(own, row_parts, inverse):
+    parts = len(row_parts)
+    rows, width = row_parts[0].shape
     side = inverse.shape[-1]
-    chunk = rows // 4
-    rows_spec = pl.BlockSpec((chunk, width), lambda i, *_: (i, 0))
+    vmem = pl.BlockSpec(memory_space=pltpu.VMEM)
     return pl.pallas_call(
         renew_kernel,
-        grid_spec=pltpu.PrefetchScalarGridSpec(
-            num_scalar_prefetch=1,
-            grid=(rows // chunk,),
-            in_specs=[rows_spec] * parts
-            + [pl.BlockSpec((parts, parts, side, side), lambda i, *_: (0, 0, 0, 0))],
-            out_specs=pl.BlockSpec((chunk, side), lambda i, *_: (i, 0)),
-        ),
-        out_shape=jax.ShapeDtypeStruct((rows, side), jnp.bfloat16),
+        in_specs=[pl.BlockSpec(memory_space=pltpu.SMEM)] + [vmem] * (parts + 1),
+        out_specs=vmem,
+        out_shape=jax.ShapeDtypeStruct((parts, rows, side), jnp.bfloat16),
         compiler_params=pltpu.CompilerParams(vmem_limit_bytes=16 * MIB),
         cost_estimate=pl.CostEstimate(
-            flops=2 * parts * rows * width * side, bytes_accessed=6 * MIB, transcendentals=0
+            flops=2 * parts * parts * rows * width * side,
+            bytes_accessed=2 * MIB,
+            transcendentals=0,
         ),
         name="renew",
-    )(own, *vectors, inverse)
+    )(own, *row_parts, inverse)
 
 
 def around(parts, step):
     return [(i, (i + step) % parts) for i in range(parts)]
-
-
-def onward(parts, step):
-    return [(i, i + step) for i in range(parts - step)]
 
 
 def body(
@@ -423,9 +470,8 @@
 
     assert side == 2 * units and units <= 256 and block_rows <= 256
     blocks = tangents.reshape(block_rows, side, width)
-    ask = jnp.concatenate([remote_owner[:, 0], remote_offset]).astype(jnp.bfloat16)
     far_count = remote_offset.shape[0]
-    pieces, spread = spread_pieces(state, gain, blocks, ask.reshape(1, width), units)
+    pieces, spread = spread_pieces(state, gain, blocks, remote_owner, remote_offset, units)
     table = lax.all_to_all(spread, "unit", 0, 0, tiled=True)
     asked = table[:, 2 * block_rows, :].astype(jnp.float32)
     index = asked[:, :far_count] * block_rows + asked[:, far_count:]
@@ -436,20 +482,16 @@
     steps = (2, 1, 3)
     assert parts == 4
     acc = local_product(local_row, local_col, local_w, pieces, blocks)
-    stepped, *outgoing = far_product(own, remote_row, remote_w, acc, arrived, parts)
+    outgoing = far_product(own, remote_row, remote_w, acc, arrived, parts)
 
     row_parts = [outgoing[0]] + [None] * 3
     for k in steps:
         row_parts[k] = lax.ppermute(outgoing[k], "vec", around(parts, k))
-    quarters = gram_quarters(own, [part.reshape(rows_dev // parts, width) for part in row_parts])
+    row_parts = [part.reshape(rows_dev // parts, width) for part in row_parts]
+    quarters = gram_quarters(own, row_parts)
     mine = quarters[0]
     for k in steps:
         mine = mine + lax.ppermute(quarters[k], "vec", around(parts, k))
-
-    late, mine = lax.optimization_barrier((stepped.reshape(rows_dev, width), mine))
-    vectors = [late] + [None] * 3
-    for k in steps:
-        vectors[k] = lax.ppermute(late, "vec", onward(parts, k))
 
     share = mine.size // units
     by_unit = lax.all_to_all(mine.reshape(units, 1, share), "unit", 0, 0, tiled=True)
@@ -461,8 +503,8 @@
         gathered[k] = lax.ppermute(quarter, "vec", around(parts, k))
 
     inverse, logs = cholesky_parts(own, gathered, unit_total)
-    renewed = renew(own, vectors, inverse)
-    return (renewed, logs.reshape(parts * width))
+    renewed = lax.all_to_all(renew(own, row_parts, inverse), "vec", 0, 0, tiled=True)
+    return (renewed.reshape(rows_dev, width), logs.reshape(parts * width))
 
 
 def solution(mesh):

time: 237 us -> 229 us (0.966)
  blocking collectives: 77.8 us -> 97.2 us
  waiting for transfers between devices: 71 us -> 61.7 us
  starting transfers between devices: 25.8 us -> 17.6 us
  local copies, waits for them, and re-layouts: 13.3 us -> 5.76 us
    all_to_all x0 -> x1, blocking collectives: none -> 17.8 us  [body(): lax.all_to_all(renew(own, row_parts, inverse), 'vec', 0, 0, tiled=True)]
    ppermute x3, waiting for transfers between devices: 17.7 us -> 7.77 us  [body(): gathered[k] = lax.ppermute(quarter, 'vec', around(parts, k))]
    ppermute x3 -> x0, starting transfers between devices: 9.15 us -> none  [body(): vectors[k] = lax.ppermute(late, 'vec', onward(parts, k))]
    unnamed x28 -> x15, local copies, waits for them, and re-layouts: 13.1 us -> 5.59 us
  transfers between devices with their start and end apart: 13 -> 10, of which waited for: 8 -> 7; matrix products, arithmetic and copies ran while one was open for 0% -> 0% of each run, Pallas kernels for 13% -> 4%
where the time goes in v2:
time: 229 us
  blocking collectives  97.2 us (42%)
  waiting for transfers between devices  61.7 us (27%)
  Pallas kernels  45.3 us (20%)
  starting transfers between devices  17.6 us (8%)
  local copies, waits for them, and re-layouts  5.76 us (3%)
    all_to_all x1, blocking collectives, body(): table = lax.all_to_all(spread, 'unit', 0, 0, tiled=True)  44.3 us
    all_to_all x1, waiting for transfers between devices, body(): arrived = lax.all_to_all(chosen, 'unit', 0, 0, tiled=True)  37 us
    pallas_call x1, Pallas kernels, cholesky_parts(): pl.pallas_call(functools.partial(factor_kernel, 1.0 / unit_total), in_spe...  22.4 us
    all_to_all x1, blocking collectives, body(): lax.all_to_all(mine.reshape(units, 1, share), 'unit', 0, 0, tiled=True)  19.3 us
    all_to_all x1, blocking collectives, body(): lax.all_to_all(renew(own, row_parts, inverse), 'vec', 0, 0, tiled=True)  17.8 us
    all_to_all x1, blocking collectives, body(): lax.all_to_all(spread_sum, 'unit', 0, 0, tiled=True).reshape(mine.shape)  15.7 us
    ppermute x3, waiting for transfers between devices, body(): row_parts[k] = lax.ppermute(outgoing[k], 'vec', around(parts, k))  11.4 us
    pallas_call x1, Pallas kernels, local_product(): pl.pallas_call(local_kernel, grid_spec=pltpu.PrefetchScalarGridSpec(num_s...  9.64 us
  transfers between devices with their start and end apart: 10, of which 7 were waited for; matrix products, arithmetic and copies ran while one was open for 0% of the time, Pallas kernels for 4%

profile of v2, /device:TPU:1, one launch (start us, length us, event | category | flops | bytes accessed | tf_op | source)
XLA Modules:
  0.0 228.6 jit_solution(10115259885433652831)
XLA Ops:
  0.6 2.1 spread_pieces.1
  2.8 44.3 %all_to_all.25.table_ref = bf16[64,72,128]{2,1,0:T(8,128)(2,1)S(1)} all-to-all(bf16[64,72,128]{2,1,0:T(8,128)(2,1)S(1)} %get-tuple-element.15), channel_id=1, replica_groups=mesh['unit'=64,'vec'=4] {'unit'}, dimensions={0} | all-to-all | bytes 2359296 | tf_op jit(solution)/shard_map/all_to_all | solution.py:475
  47.2 0.1 reshape.62.index_ref
  47.3 6.1 %pick_rows.1 = bf16[64,128,128]{2,1,0:T(8,128)(2,1)} custom-call(f32[4,8,128]{2,1,0:T(8,128)S(1)} %reshape.62.index_ref, bf16[64,72,128]{2,1,0:T(8,128)(2,1)S(1)} %all_to_all.25.table_ref), custom_call_target="tpu_custom_call" | custom-call | flops 4000000000 | bytes 4194304 | tf_op jit(solution)/shard_map/pick_rows/pallas_call | solution.py:177
  53.4 6.3 %all-to-all-start.1 = ((bf16[64,128,128]{2,1,0:T(8,128)(2,1)}), bf16[64,128,128]{2,1,0:T(8,128)(2,1)S(1)}, u32[]{:S(2)}, u32[]{:S(2)}) async-start(bf16[64,128,128]{2,1,0:T(8,128)(2,1)} %pick_rows.1), calls=%async_computation.1 | async-start | bytes 4194304 | tf_op jit(solution)/shard_map/all_to_all | solution.py:479
  59.8 3.4 %copy-done = bf16[256,128,128]{2,1,0:T(8,128)(2,1)S(1)} copy-done((bf16[256,128,128]{2,1,0:T(8,128)(2,1)S(1)}, bf16[256,128,128]{2,1,0:T(8,128)(2,1)}, u32[]{:S(2)}) %copy-start) | copy-done | bytes 8388632
  63.1 1.2 copy-done.3
  64.4 9.6 %local_blocks.1.acc_hbm = f32[32,128,128]{2,1,0:T(8,128)} custom-call(s32[256]{0:T(256)S(1)} %copy-done.4, s32[256]{0:T(256)S(1)} %copy-done.5, bf16[256,128,128]{2,1,0:T(8,128)(2,1)S(1)} %copy-done, bf16[32,128,128]{2,1,0:T(8,128)(2,1)S(1)} %copy-done.3, bf16[32,128,128]{2,1,0:T(8,128)(2,1)S(1)} %bitcast.16), custom_call_target="tpu_custom_call" | custom-call | flops 1073741824 | bytes 14680064 | tf_op jit(solution)/shard_map/local_blocks/pallas_call | solution.py:47
  74.0 37.0 %all-to-all-done.1.arrived_ref = bf16[64,128,128]{2,1,0:T(8,128)(2,1)S(1)} async-done(((bf16[64,128,128]{2,1,0:T(8,128)(2,1)}), bf16[64,128,128]{2,1,0:T(8,128)(2,1)S(1)}, u32[]{:S(2)}, u32[]{:S(2)}) %all-to-all-start.1) | async-done | bytes 2097184 | tf_op jit(solution)/shard_map/all_to_all | solution.py:479
  111.0 3.0 %far_blocks.1 = (bf16[8,128,128]{2,1,0:T(8,128)(2,1)S(1)}, bf16[8,128,128]{2,1,0:T(8,128)(2,1)S(1)}, bf16[8,128,128]{2,1,0:T(8,128)(2,1)S(1)}, bf16[8,128,128]{2,1,0:T(8,128)(2,1)S(1)}) custom-call(s32[1]{0:T(128)} %bitcast.own_ref, s32[64]{0:T(128)S(1)} %copy-done.6, bf16[64,128,128]{2,1,0:T(8,128)(2,1)} %w_hbm.1, f32[32,128,128]{2,1,0:T(8,128)} %local_blocks.1.acc_hbm, ...), custom_call_target="tpu_custom_call" | custom-call | flops 268435456 | bytes 8388608 | tf_op jit(solution)/shard_map/far_blocks/pallas_call | solution.py:236
  114.0 2.6 %collective-permute-start.2 = (bf16[8,128,128]{2,1,0:T(8,128)(2,1)S(1)}, bf16[8,128,128]{2,1,0:T(8,128)(2,1)S(1)}, u32[]{:S(2)}, u32[]{:S(2)}) collective-permute-start(bf16[8,128,128]{2,1,0:T(8,128)(2,1)S(1)} %get-tuple-element.19), channel_id=1, source_target_pairs={{0,3},{1,0},{2,1},{3,2},{4,7},{5,4},{6,5},{7,6},{8,11},{9,8},{10,9... | collective-permute-start | bytes 786440 | tf_op jit(solution)/shard_map/ppermute | solution.py:489
  116.5 1.7 collective-permute-start.1
  118.3 9.0 %collective-permute-done.2 = bf16[8,128,128]{2,1,0:T(8,128)(2,1)S(1)} collective-permute-done((bf16[8,128,128]{2,1,0:T(8,128)(2,1)S(1)}, bf16[8,128,128]{2,1,0:T(8,128)(2,1)S(1)}, u32[]{:S(2)}, u32[]{:S(2)}) %collective-permute-start.2) | collective-permute-done | bytes 262176 | tf_op jit(solution)/shard_map/ppermute | solution.py:489
  127.3 2.3 %collective-permute-done.1 = bf16[8,128,128]{2,1,0:T(8,128)(2,1)S(1)} collective-permute-done((bf16[8,128,128]{2,1,0:T(8,128)(2,1)S(1)}, bf16[8,128,128]{2,1,0:T(8,128)(2,1)S(1)}, u32[]{:S(2)}, u32[]{:S(2)}) %collective-permute-start.1) | collective-permute-done | bytes 262176 | tf_op jit(solution)/shard_map/ppermute | solution.py:489
  129.6 0.8 gram_quarters.1
  130.5 1.6 collective-permute-start.3
  132.1 0.3 collective-permute-start.4
  132.4 2.4 %collective-permute-start.5 = (f32[320,128]{1,0:T(8,128)S(1)}, f32[320,128]{1,0:T(8,128)S(1)}, u32[]{:S(2)}, u32[]{:S(2)}) collective-permute-start(f32[320,128]{1,0:T(8,128)S(1)} %get-tuple-element.23), channel_id=1, source_target_pairs={{0,3},{1,0},{2,1},{3,2},{4,7},{5,4},{6,5},{7,6},{8,11},{9,8},{10,9... | collective-permute-start | bytes 491528 | tf_op jit(solution)/shard_map/ppermute | solution.py:494
  134.7 1.5 collective-permute-done.3
  136.3 4.1 %collective-permute-done.4 = f32[320,128]{1,0:T(8,128)S(1)} collective-permute-done((f32[320,128]{1,0:T(8,128)S(1)}, f32[320,128]{1,0:T(8,128)S(1)}, u32[]{:S(2)}, u32[]{:S(2)}) %collective-permute-start.4) | collective-permute-done | bytes 163872 | tf_op jit(solution)/shard_map/ppermute | solution.py:494
  140.4 19.3 %all_to_all.26 = f32[64,1,640]{2,1,0:T(1,128)S(1)} all-to-all(f32[64,1,640]{2,1,0:T(1,128)S(1)} %bitcast.30), channel_id=1, replica_groups=mesh['unit'=64,'vec'=4] {'unit'}, dimensions={0} | all-to-all | bytes 327680 | tf_op jit(solution)/shard_map/all_to_all | solution.py:497
  159.7 0.1 reduce_sum.9
  159.9 0.1 broadcast_in_dim.2
  160.0 15.7 %all_to_all.27 = f32[64,1,640]{2,1,0:T(1,128)S(1)} all-to-all(f32[64,1,640]{2,1,0:T(1,128)S(1)} %broadcast_in_dim.2), channel_id=1, replica_groups=mesh['unit'=64,'vec'=4] {'unit'}, dimensions={0} | all-to-all | bytes 327680 | tf_op jit(solution)/shard_map/all_to_all | solution.py:500
  175.7 1.7 collective-permute-start.7
  177.4 1.0 collective-permute-start.8
  178.4 7.4 %collective-permute-done.6.refs_1_ = f32[320,128]{1,0:T(8,128)S(1)} collective-permute-done((f32[320,128]{1,0:T(8,128)S(1)}, f32[320,128]{1,0:T(8,128)S(1)}, u32[]{:S(2)}, u32[]{:S(2)}) %collective-permute-start.6) | collective-permute-done | bytes 163872 | tf_op jit(solution)/shard_map/ppermute | solution.py:503
  185.8 0.3 collective-permute-done.8.refs_3_
  186.2 22.4 %factor.1 = (bf16[4,4,128,128]{3,2,1,0:T(8,128)(2,1)S(1)}, f32[4,128]{1,0:T(4,128)}) custom-call(s32[1]{0:T(128)} %bitcast.own_ref, f32[320,128]{1,0:T(8,128)S(1)} %bitcast.28, f32[320,128]{1,0:T(8,128)S(1)} %collective-permute-done.6.refs_1_, f32[320,128]{1,0:T(8,128)S(1)} %collective-permute-done.7.refs_2_, f32[320,128]{1,0:T(8,128)S(1)} %collective-permute-done.8.refs_3_), custom_call_target="tpu_custom_call" | custom-call | flops 200000000 | bytes 2097152 | tf_op jit(solution)/shard_map/factor/pallas_call | solution.py:391
  208.5 1.2 renew.1
  209.8 17.8 %all_to_all.28 = bf16[4,1024,128]{2,1,0:T(8,128)(2,1)S(1)} all-to-all(bf16[4,1024,128]{2,1,0:T(8,128)(2,1)S(1)} %renew.1), channel_id=1, replica_groups=mesh['unit'=64,'vec'=4] {'vec'}, dimensions={0} | all-to-all | bytes 2097152 | tf_op jit(solution)/shard_map/all_to_all | solution.py:506
  227.6 1.0 copy.14
  (20 shorter events, 0.2 us)
Async XLA Ops:
  2.8 44.3 %copy-start.2 = (bf16[32,128,128]{2,1,0:T(8,128)(2,1)}, bf16[32,128,128]{2,1,0:T(8,128)(2,1)S(1)}, u32[]{:S(2)}) copy-start(bf16[32,128,128]{2,1,0:T(8,128)(2,1)S(1)} %get-tuple-element.14.x_ref) | copy-start | bytes 3145732
  53.4 6.3 %copy-start.1 = (bf16[4096,128]{1,0:T(8,128)(2,1)S(1)}, bf16[4096,128]{1,0:T(8,128)(2,1)}, u32[]{:S(2)}) copy-start(bf16[4096,128]{1,0:T(8,128)(2,1)} %param.10) | copy-start | bytes 3145732
  53.4 6.4 %copy-start.4 = (s32[256]{0:T(256)S(1)}, s32[256]{0:T(256)}, u32[]{:S(2)}) copy-start(s32[256]{0:T(256)} %row_ref.2) | copy-start | bytes 3076
  53.4 6.4 %copy-start.5 = (s32[256]{0:T(256)S(1)}, s32[256]{0:T(256)}, u32[]{:S(2)}) copy-start(s32[256]{0:T(256)} %col_ref.1) | copy-start | bytes 3076
  53.4 57.6 %all-to-all-start.1 = ((bf16[64,128,128]{2,1,0:T(8,128)(2,1)}), bf16[64,128,128]{2,1,0:T(8,128)(2,1)S(1)}, u32[]{:S(2)}, u32[]{:S(2)}) async-start(bf16[64,128,128]{2,1,0:T(8,128)(2,1)} %pick_rows.1), calls=%async_computation.1 | async-start | bytes 4194304 | tf_op jit(solution)/shard_map/all_to_all | solution.py:479
  59.7 3.4 %copy-start = (bf16[256,128,128]{2,1,0:T(8,128)(2,1)S(1)}, bf16[256,128,128]{2,1,0:T(8,128)(2,1)}, u32[]{:S(2)}) copy-start(bf16[256,128,128]{2,1,0:T(8,128)(2,1)} %w_ref.1) | copy-start | bytes 25165828
  63.1 1.2 copy-start.3
  64.4 46.6 %copy-start.6 = (s32[64]{0:T(128)S(1)}, s32[64]{0:T(128)}, u32[]{:S(2)}) copy-start(s32[64]{0:T(128)} %row_ref.3) | copy-start | bytes 772
  114.0 13.3 %collective-permute-start.2 = (bf16[8,128,128]{2,1,0:T(8,128)(2,1)S(1)}, bf16[8,128,128]{2,1,0:T(8,128)(2,1)S(1)}, u32[]{:S(2)}, u32[]{:S(2)}) collective-permute-start(bf16[8,128,128]{2,1,0:T(8,128)(2,1)S(1)} %get-tuple-element.19), channel_id=1, source_target_pairs={{0,3},{1,0},{2,1},{3,2},{4,7},{5,4},{6,5},{7,6},{8,11},{9,8},{10,9... | collective-permute-start | bytes 786440 | tf_op jit(solution)/shard_map/ppermute | solution.py:489
  116.5 10.8 %collective-permute-start = (bf16[8,128,128]{2,1,0:T(8,128)(2,1)S(1)}, bf16[8,128,128]{2,1,0:T(8,128)(2,1)S(1)}, u32[]{:S(2)}, u32[]{:S(2)}) collective-permute-start(bf16[8,128,128]{2,1,0:T(8,128)(2,1)S(1)} %get-tuple-element.17), channel_id=1, source_target_pairs={{0,1},{1,2},{2,3},{3,0},{4,5},{5,6},{6,7},{7,4},{8,9},{9,10},{10,1... | collective-permute-start | bytes 786440 | tf_op jit(solution)/shard_map/ppermute | solution.py:489
  116.5 13.1 %collective-permute-start.1 = (bf16[8,128,128]{2,1,0:T(8,128)(2,1)S(1)}, bf16[8,128,128]{2,1,0:T(8,128)(2,1)S(1)}, u32[]{:S(2)}, u32[]{:S(2)}) collective-permute-start(bf16[8,128,128]{2,1,0:T(8,128)(2,1)S(1)} %get-tuple-element.18), channel_id=1, source_target_pairs={{0,2},{1,3},{2,0},{3,1},{4,6},{5,7},{6,4},{7,5},{8,10},{9,11},{10,... | collective-permute-start | bytes 786440 | tf_op jit(solution)/shard_map/ppermute | solution.py:489
  130.5 5.8 %collective-permute-start.3 = (f32[320,128]{1,0:T(8,128)S(1)}, f32[320,128]{1,0:T(8,128)S(1)}, u32[]{:S(2)}, u32[]{:S(2)}) collective-permute-start(f32[320,128]{1,0:T(8,128)S(1)} %get-tuple-element.21), channel_id=1, source_target_pairs={{0,2},{1,3},{2,0},{3,1},{4,6},{5,7},{6,4},{7,5},{8,10},{9,11},{10,... | collective-permute-start | bytes 491528 | tf_op jit(solution)/shard_map/ppermute | solution.py:494
  132.1 8.3 %collective-permute-start.4 = (f32[320,128]{1,0:T(8,128)S(1)}, f32[320,128]{1,0:T(8,128)S(1)}, u32[]{:S(2)}, u32[]{:S(2)}) collective-permute-start(f32[320,128]{1,0:T(8,128)S(1)} %get-tuple-element.22), channel_id=1, source_target_pairs={{0,1},{1,2},{2,3},{3,0},{4,5},{5,6},{6,7},{7,4},{8,9},{9,10},{10,1... | collective-permute-start | bytes 491528 | tf_op jit(solution)/shard_map/ppermute | solution.py:494
  132.4 8.0 %collective-permute-start.5 = (f32[320,128]{1,0:T(8,128)S(1)}, f32[320,128]{1,0:T(8,128)S(1)}, u32[]{:S(2)}, u32[]{:S(2)}) collective-permute-start(f32[320,128]{1,0:T(8,128)S(1)} %get-tuple-element.23), channel_id=1, source_target_pairs={{0,3},{1,0},{2,1},{3,2},{4,7},{5,4},{6,5},{7,6},{8,11},{9,8},{10,9... | collective-permute-start | bytes 491528 | tf_op jit(solution)/shard_map/ppermute | solution.py:494
  175.7 10.1 %collective-permute-start.6 = (f32[320,128]{1,0:T(8,128)S(1)}, f32[320,128]{1,0:T(8,128)S(1)}, u32[]{:S(2)}, u32[]{:S(2)}) collective-permute-start(f32[320,128]{1,0:T(8,128)S(1)} %bitcast.25), channel_id=1, source_target_pairs={{0,1},{1,2},{2,3},{3,0},{4,5},{5,6},{6,7},{7,4},{8,9},{9,10},{10,1... | collective-permute-start | bytes 491528 | tf_op jit(solution)/shard_map/ppermute | solution.py:503
  175.7 10.1 %collective-permute-start.7 = (f32[320,128]{1,0:T(8,128)S(1)}, f32[320,128]{1,0:T(8,128)S(1)}, u32[]{:S(2)}, u32[]{:S(2)}) collective-permute-start(f32[320,128]{1,0:T(8,128)S(1)} %bitcast.26), channel_id=1, source_target_pairs={{0,2},{1,3},{2,0},{3,1},{4,6},{5,7},{6,4},{7,5},{8,10},{9,11},{10,... | collective-permute-start | bytes 491528 | tf_op jit(solution)/shard_map/ppermute | solution.py:503
  177.4 8.7 %collective-permute-start.8 = (f32[320,128]{1,0:T(8,128)S(1)}, f32[320,128]{1,0:T(8,128)S(1)}, u32[]{:S(2)}, u32[]{:S(2)}) collective-permute-start(f32[320,128]{1,0:T(8,128)S(1)} %bitcast.27), channel_id=1, source_target_pairs={{0,3},{1,0},{2,1},{3,2},{4,7},{5,4},{6,5},{7,6},{8,11},{9,8},{10,9... | collective-permute-start | bytes 491528 | tf_op jit(solution)/shard_map/ppermute | solution.py:503

commit v3 on v2

--- a/solution.py
+++ b/solution.py
@@ -192,7 +192,7 @@
 
 
 def far_kernel(own_ref, row_ref, w_hbm, acc_hbm, arrived_ref, *rest):
-    part_refs, (far_ref, acc_ref, w_ref, x_ref, sems) = rest[:-5], rest[-5:]
+    whole_ref, part_refs, (far_ref, acc_ref, w_ref, x_ref, sems) = rest[0], rest[1:-5], rest[-5:]
     count = w_ref.shape[0]
     units = arrived_ref.shape[0]
     groups = count // 16
@@ -224,7 +224,9 @@
     for k in range(parts):
         share = part_refs[k].shape[0]
         here = pl.ds(lax.rem(own_ref[0] + k, parts) * share, share)
-        part_refs[k][...] = (time_step * (acc_ref[here] + far_ref[here])).astype(jnp.bfloat16)
+        stepped = (time_step * (acc_ref[here] + far_ref[here])).astype(jnp.bfloat16)
+        part_refs[k][...] = stepped
+        whole_ref[here] = stepped
 
 
 def far_product(own, remote_row, remote_w, acc, arrived, parts):
@@ -236,8 +238,9 @@
     return pl.pallas_call(
         far_kernel,
         in_specs=[smem, smem, hbm, hbm, vmem],
-        out_specs=[vmem] * parts,
-        out_shape=[jax.ShapeDtypeStruct((block_rows // parts, side, width), jnp.bfloat16)] * parts,
+        out_specs=[vmem] * (1 + parts),
+        out_shape=[jax.ShapeDtypeStruct((block_rows, side, width), jnp.bfloat16)]
+        + [jax.ShapeDtypeStruct((block_rows // parts, side, width), jnp.bfloat16)] * parts,
         scratch_shapes=[
             pltpu.VMEM((block_rows, side, width), jnp.float32),
             pltpu.VMEM((block_rows, side, width), jnp.float32),
@@ -409,40 +412,47 @@
 
 
 def renew_kernel(own_ref, *refs):
-    x_refs, (inv_ref, out_ref) = refs[:-2], refs[-2:]
+    x_refs, (inv_ref, out_hbm, out_ref, sems) = refs[:-4], refs[-4:]
     own = own_ref[0]
     parts = len(x_refs)
-    for b in range(parts):
-        total = None
-        for k in range(parts):
-            term = lax.dot_general(
-                x_refs[k][...],
-                inv_ref[b, lax.rem(own + parts - k, parts)],
-                (((1,), (1,)), ((), ())),
-                preferred_element_type=jnp.float32,
-            )
-            total = term if total is None else total + term
-        out_ref[b] = total.astype(jnp.bfloat16)
-
-
-def renew(own, row_parts, inverse):
-    parts = len(row_parts)
-    rows, width = row_parts[0].shape
+    chunks = sems.shape[0]
+    chunk = out_ref.shape[0] // chunks
+    inverse = jnp.concatenate(
+        [inv_ref[own, lax.rem(own + parts - k, parts)] for k in range(parts)], axis=1
+    )
+    copies = []
+    for c in range(chunks):
+        here = pl.ds(c * chunk, chunk)
+        vectors = jnp.concatenate([x_ref[here, :] for x_ref in x_refs], axis=1)
+        out_ref[here, :] = lax.dot_general(
+            vectors, inverse, (((1,), (1,)), ((), ())), preferred_element_type=jnp.float32
+        ).astype(jnp.bfloat16)
+        copies.append(pltpu.make_async_copy(out_ref.at[here], out_hbm.at[here], sems.at[c]))
+        copies[c].start()
+    for copy in copies:
+        copy.wait()
+
+
+def renew(own, vectors, inverse):
+    parts = len(vectors)
+    rows, width = vectors[0].shape
     side = inverse.shape[-1]
     vmem = pl.BlockSpec(memory_space=pltpu.VMEM)
     return pl.pallas_call(
         renew_kernel,
         in_specs=[pl.BlockSpec(memory_space=pltpu.SMEM)] + [vmem] * (parts + 1),
-        out_specs=vmem,
-        out_shape=jax.ShapeDtypeStruct((parts, rows, side), jnp.bfloat16),
+        out_specs=pl.BlockSpec(memory_space=pltpu.HBM),
+        out_shape=pltpu.HBM((rows, side), jnp.bfloat16),
+        scratch_shapes=[
+            pltpu.VMEM((rows, side), jnp.bfloat16),
+            pltpu.SemaphoreType.DMA((4,)),
+        ],
         compiler_params=pltpu.CompilerParams(vmem_limit_bytes=16 * MIB),
         cost_estimate=pl.CostEstimate(
-            flops=2 * parts * parts * rows * width * side,
-            bytes_accessed=2 * MIB,
-            transcendentals=0,
+            flops=2 * parts * rows * width * side, bytes_accessed=6 * MIB, transcendentals=0
         ),
         name="renew",
-    )(own, *row_parts, inverse)
+    )(own, *vectors, inverse)
 
 
 def around(parts, step):
@@ -482,7 +492,7 @@
     steps = (2, 1, 3)
     assert parts == 4
     acc = local_product(local_row, local_col, local_w, pieces, blocks)
-    outgoing = far_product(own, remote_row, remote_w, acc, arrived, parts)
+    stepped, *outgoing = far_product(own, remote_row, remote_w, acc, arrived, parts)
 
     row_parts = [outgoing[0]] + [None] * 3
     for k in steps:
@@ -493,18 +503,26 @@
     for k in steps:
         mine = mine + lax.ppermute(quarters[k], "vec", around(parts, k))
 
+    late, mine = lax.optimization_barrier((stepped.reshape(rows_dev, width), mine))
+    vectors = [late] + [None] * 3
+    for k in (1, 3):
+        vectors[k] = lax.ppermute(late, "vec", around(parts, k))
+
     share = mine.size // units
     by_unit = lax.all_to_all(mine.reshape(units, 1, share), "unit", 0, 0, tiled=True)
     summed = jnp.sum(by_unit, axis=0, keepdims=True)
     spread_sum = jnp.broadcast_to(summed, (units, 1, share))
     quarter = lax.all_to_all(spread_sum, "unit", 0, 0, tiled=True).reshape(mine.shape)
+    quarter, vectors[1], vectors[3] = lax.optimization_barrier((quarter, vectors[1], vectors[3]))
     gathered = [quarter] + [None] * 3
     for k in steps:
         gathered[k] = lax.ppermute(quarter, "vec", around(parts, k))
 
+    later, gathered = lax.optimization_barrier((late, gathered))
+    vectors[2] = lax.ppermute(later, "vec", around(parts, 2))
     inverse, logs = cholesky_parts(own, gathered, unit_total)
-    renewed = lax.all_to_all(renew(own, row_parts, inverse), "vec", 0, 0, tiled=True)
-    return (renewed.reshape(rows_dev, width), logs.reshape(parts * width))
+    renewed = renew(own, vectors, inverse)
+    return (renewed, logs.reshape(parts * width))
 
 
 def solution(mesh):

time: 229 us -> 219 us (0.956)
  blocking collectives: 97.2 us -> 77.5 us
  starting transfers between devices: 17.6 us -> 23 us
  waiting for transfers between devices: 61.7 us -> 65.6 us
    all_to_all x1 -> x0, blocking collectives: 17.8 us -> none  [body(): lax.all_to_all(renew(own, row_parts, inverse), 'vec', 0, 0, tiled=True)]
    ppermute x0 -> x3, starting transfers between devices: none -> 3.26 us  [the longest x2 2.67 us: body(): vectors[k] = lax.ppermute(late, 'vec', around(parts, k))]
    ppermute x0 -> x3, waiting for transfers between devices: none -> 2.43 us  [the longest x1 2.43 us: body(): vectors[2] = lax.ppermute(later, 'vec', around(parts, 2))]
    unnamed x15 -> x14, local copies, waits for them, and re-layouts: 5.59 us -> 4.62 us
  transfers between devices with their start and end apart: 10 -> 13, of which waited for: 7 -> 10; matrix products, arithmetic and copies ran while one was open for 0% -> 0% of each run, Pallas kernels for 4% -> 15%
where the time goes in v3:
time: 219 us; the launch traced here: 218 us
  blocking collectives  77.5 us (35%)
  waiting for transfers between devices  65.6 us (30%)
  Pallas kernels  46.2 us (21%)
  starting transfers between devices  23 us (11%)
  local copies, waits for them, and re-layouts  4.79 us (2%)
    all_to_all x1, blocking collectives, body(): table = lax.all_to_all(spread, 'unit', 0, 0, tiled=True)  44.3 us
    all_to_all x1, waiting for transfers between devices, body(): arrived = lax.all_to_all(chosen, 'unit', 0, 0, tiled=True)  37 us
    pallas_call x1, Pallas kernels, cholesky_parts(): pl.pallas_call(functools.partial(factor_kernel, 1.0 / unit_total), in_spe...  22.4 us
    all_to_all x1, blocking collectives, body(): lax.all_to_all(mine.reshape(units, 1, share), 'unit', 0, 0, tiled=True)  17.4 us
    all_to_all x1, blocking collectives, body(): lax.all_to_all(spread_sum, 'unit', 0, 0, tiled=True).reshape(mine.shape)  15.7 us
    ppermute x3, waiting for transfers between devices, body(): row_parts[k] = lax.ppermute(outgoing[k], 'vec', around(parts, k))  10.5 us
    ppermute x3, waiting for transfers between devices, body(): gathered[k] = lax.ppermute(quarter, 'vec', around(parts, k))  9.87 us
    pallas_call x1, Pallas kernels, local_product(): pl.pallas_call(local_kernel, grid_spec=pltpu.PrefetchScalarGridSpec(num_s...  9.62 us
  transfers between devices with their start and end apart: 13, of which 10 were waited for; matrix products, arithmetic and copies ran while one was open for 0% of the time, Pallas kernels for 15%

profile of v3, /device:TPU:1, one launch (start us, length us, event | category | flops | bytes accessed | tf_op | source)
XLA Modules:
  0.0 218.2 jit_solution(11300002641141133758)
XLA Ops:
  0.6 2.1 spread_pieces.1
  2.8 44.3 %all_to_all.20.table_ref = bf16[64,72,128]{2,1,0:T(8,128)(2,1)S(1)} all-to-all(bf16[64,72,128]{2,1,0:T(8,128)(2,1)S(1)} %get-tuple-element.26), channel_id=1, replica_groups=mesh['unit'=64,'vec'=4] {'unit'}, dimensions={0} | all-to-all | bytes 2359296 | tf_op jit(solution)/shard_map/all_to_all | solution.py:485
  47.3 6.1 %pick_rows.1 = bf16[64,128,128]{2,1,0:T(8,128)(2,1)} custom-call(f32[4,8,128]{2,1,0:T(8,128)S(1)} %reshape.62.index_ref, bf16[64,72,128]{2,1,0:T(8,128)(2,1)S(1)} %all_to_all.20.table_ref), custom_call_target="tpu_custom_call" | custom-call | flops 4000000000 | bytes 4194304 | tf_op jit(solution)/shard_map/pick_rows/pallas_call | solution.py:177
  53.4 6.3 %all-to-all-start.1 = ((bf16[64,128,128]{2,1,0:T(8,128)(2,1)}), bf16[64,128,128]{2,1,0:T(8,128)(2,1)S(1)}, u32[]{:S(2)}, u32[]{:S(2)}) async-start(bf16[64,128,128]{2,1,0:T(8,128)(2,1)} %pick_rows.1), calls=%async_computation.1 | async-start | bytes 4194304 | tf_op jit(solution)/shard_map/all_to_all | solution.py:489
  59.7 3.4 %copy-done = bf16[256,128,128]{2,1,0:T(8,128)(2,1)S(1)} copy-done((bf16[256,128,128]{2,1,0:T(8,128)(2,1)S(1)}, bf16[256,128,128]{2,1,0:T(8,128)(2,1)}, u32[]{:S(2)}) %copy-start) | copy-done | bytes 8388632
  63.1 1.2 copy-done.3
  64.3 9.6 %local_blocks.1.acc_hbm = f32[32,128,128]{2,1,0:T(8,128)} custom-call(s32[256]{0:T(256)S(1)} %copy-done.4, s32[256]{0:T(256)S(1)} %copy-done.5, bf16[256,128,128]{2,1,0:T(8,128)(2,1)S(1)} %copy-done, bf16[32,128,128]{2,1,0:T(8,128)(2,1)S(1)} %copy-done.3, bf16[32,128,128]{2,1,0:T(8,128)(2,1)S(1)} %bitcast.16), custom_call_target="tpu_custom_call" | custom-call | flops 1073741824 | bytes 14680064 | tf_op jit(solution)/shard_map/local_blocks/pallas_call | solution.py:47
  74.0 37.0 %all-to-all-done.1.arrived_ref = bf16[64,128,128]{2,1,0:T(8,128)(2,1)S(1)} async-done(((bf16[64,128,128]{2,1,0:T(8,128)(2,1)}), bf16[64,128,128]{2,1,0:T(8,128)(2,1)S(1)}, u32[]{:S(2)}, u32[]{:S(2)}) %all-to-all-start.1) | async-done | bytes 2097184 | tf_op jit(solution)/shard_map/all_to_all | solution.py:489
  110.9 3.1 %far_blocks.1 = (bf16[32,128,128]{2,1,0:T(8,128)(2,1)S(1)}, bf16[8,128,128]{2,1,0:T(8,128)(2,1)S(1)}, bf16[8,128,128]{2,1,0:T(8,128)(2,1)S(1)}, bf16[8,128,128]{2,1,0:T(8,128)(2,1)S(1)}, bf16[8,128,128]{2,1,0:T(8,128)(2,1)S(1)}) custom-call(s32[1]{0:T(128)} %bitcast.own_ref, s32[64]{0:T(128)S(1)} %copy-done.6, bf16[64,128,128]{2,1,0:T(8,128)(2,1)} %w_hbm.1, ...), custom_call_target="tpu_custom_call" | custom-call | flops 268435456 | bytes 8388608 | tf_op jit(solution)/shard_map/far_blocks/pallas_call | solution.py:238
  114.0 1.3 collective-permute-start
  115.3 2.4 %collective-permute-start.1 = (bf16[8,128,128]{2,1,0:T(8,128)(2,1)S(1)}, bf16[8,128,128]{2,1,0:T(8,128)(2,1)S(1)}, u32[]{:S(2)}, u32[]{:S(2)}) collective-permute-start(bf16[8,128,128]{2,1,0:T(8,128)(2,1)S(1)} %get-tuple-element.30), channel_id=1, source_target_pairs={{0,2},{1,3},{2,0},{3,1},{4,6},{5,7},{6,4},{7,5},{8,10},{9,11},{10,... | collective-permute-start | bytes 786440 | tf_op jit(solution)/shard_map/ppermute | solution.py:499
  117.7 1.2 collective-permute-start.2
  118.9 3.9 %collective-permute-done = bf16[8,128,128]{2,1,0:T(8,128)(2,1)S(1)} collective-permute-done((bf16[8,128,128]{2,1,0:T(8,128)(2,1)S(1)}, bf16[8,128,128]{2,1,0:T(8,128)(2,1)S(1)}, u32[]{:S(2)}, u32[]{:S(2)}) %collective-permute-start) | collective-permute-done | bytes 262176 | tf_op jit(solution)/shard_map/ppermute | solution.py:499
  122.8 6.6 %collective-permute-done.1 = bf16[8,128,128]{2,1,0:T(8,128)(2,1)S(1)} collective-permute-done((bf16[8,128,128]{2,1,0:T(8,128)(2,1)S(1)}, bf16[8,128,128]{2,1,0:T(8,128)(2,1)S(1)}, u32[]{:S(2)}, u32[]{:S(2)}) %collective-permute-start.1) | collective-permute-done | bytes 262176 | tf_op jit(solution)/shard_map/ppermute | solution.py:499
  129.4 0.8 gram_quarters.1
  130.2 2.2 %collective-permute-start.3 = (f32[320,128]{1,0:T(8,128)S(1)}, f32[320,128]{1,0:T(8,128)S(1)}, u32[]{:S(2)}, u32[]{:S(2)}) collective-permute-start(f32[320,128]{1,0:T(8,128)S(1)} %get-tuple-element.33), channel_id=1, source_target_pairs={{0,2},{1,3},{2,0},{3,1},{4,6},{5,7},{6,4},{7,5},{8,10},{9,11},{10,... | collective-permute-start | bytes 491528 | tf_op jit(solution)/shard_map/ppermute | solution.py:504
  132.4 1.2 collective-permute-start.4
  133.6 1.5 collective-permute-start.5
  135.1 0.9 collective-permute-done.3
  136.0 4.4 %collective-permute-done.4 = f32[320,128]{1,0:T(8,128)S(1)} collective-permute-done((f32[320,128]{1,0:T(8,128)S(1)}, f32[320,128]{1,0:T(8,128)S(1)}, u32[]{:S(2)}, u32[]{:S(2)}) %collective-permute-start.4) | collective-permute-done | bytes 163872 | tf_op jit(solution)/shard_map/ppermute | solution.py:504
  140.4 0.5 collective-permute-done.5
  141.0 2.7 %collective-permute-start.7 = (bf16[4096,128]{1,0:T(8,128)(2,1)S(1)}, bf16[4096,128]{1,0:T(8,128)(2,1)S(1)}, u32[]{:S(2)}, u32[]{:S(2)}) collective-permute-start(bf16[4096,128]{1,0:T(8,128)(2,1)S(1)} %bitcast.17), channel_id=1, source_target_pairs={{0,3},{1,0},{2,1},{3,2},{4,7},{5,4},{6,5},{7,6},{8,11},{9,8},{10,9... | collective-permute-start | bytes 3145736 | tf_op jit(solution)/shard_map/ppermute | solution.py:509
  143.7 17.4 %all_to_all.21 = f32[64,1,640]{2,1,0:T(1,128)S(1)} all-to-all(f32[64,1,640]{2,1,0:T(1,128)S(1)} %bitcast.29), channel_id=1, replica_groups=mesh['unit'=64,'vec'=4] {'unit'}, dimensions={0} | all-to-all | bytes 327680 | tf_op jit(solution)/shard_map/all_to_all | solution.py:512
  161.3 15.7 %all_to_all.22 = f32[64,1,640]{2,1,0:T(1,128)S(1)} all-to-all(f32[64,1,640]{2,1,0:T(1,128)S(1)} %broadcast_in_dim.2), channel_id=1, replica_groups=mesh['unit'=64,'vec'=4] {'unit'}, dimensions={0} | all-to-all | bytes 327680 | tf_op jit(solution)/shard_map/all_to_all | solution.py:515
  177.1 3.0 %collective-permute-start.10 = (f32[320,128]{1,0:T(8,128)S(1)}, f32[320,128]{1,0:T(8,128)S(1)}, u32[]{:S(2)}, u32[]{:S(2)}) collective-permute-start(f32[320,128]{1,0:T(8,128)S(1)} %bitcast.21), channel_id=1, source_target_pairs={{0,3},{1,0},{2,1},{3,2},{4,7},{5,4},{6,5},{7,6},{8,11},{9,8},{10,9... | collective-permute-start | bytes 491528 | tf_op jit(solution)/shard_map/ppermute | solution.py:519
  180.0 0.7 collective-permute-start.8
  180.7 5.9 %collective-permute-done.10.refs_3_ = f32[320,128]{1,0:T(8,128)S(1)} collective-permute-done((f32[320,128]{1,0:T(8,128)S(1)}, f32[320,128]{1,0:T(8,128)S(1)}, u32[]{:S(2)}, u32[]{:S(2)}) %collective-permute-start.10) | collective-permute-done | bytes 163872 | tf_op jit(solution)/shard_map/ppermute | solution.py:519
  186.7 3.9 %collective-permute-done.8.refs_1_ = f32[320,128]{1,0:T(8,128)S(1)} collective-permute-done((f32[320,128]{1,0:T(8,128)S(1)}, f32[320,128]{1,0:T(8,128)S(1)}, u32[]{:S(2)}, u32[]{:S(2)}) %collective-permute-start.8) | collective-permute-done | bytes 163872 | tf_op jit(solution)/shard_map/ppermute | solution.py:519
  190.5 0.6 collective-permute-start.11
  191.1 22.4 %factor.1 = (bf16[4,4,128,128]{3,2,1,0:T(8,128)(2,1)S(1)}, f32[4,128]{1,0:T(4,128)}) custom-call(s32[1]{0:T(128)} %bitcast.own_ref, f32[320,128]{1,0:T(8,128)S(1)} %bitcast.24, f32[320,128]{1,0:T(8,128)S(1)} %collective-permute-done.8.refs_1_, f32[320,128]{1,0:T(8,128)S(1)} %collective-permute-done.9.refs_2_, f32[320,128]{1,0:T(8,128)S(1)} %collective-permute-done.10.refs_3_), custom_call_target="tpu_custom_call" | custom-call | flops 200000000 | bytes 2097152 | tf_op jit(solution)/shard_map/factor/pallas_call | solution.py:394
  213.5 2.4 %collective-permute-done.11.refs_2_ = bf16[4096,128]{1,0:T(8,128)(2,1)S(1)} collective-permute-done((bf16[4096,128]{1,0:T(8,128)(2,1)S(1)}, bf16[4096,128]{1,0:T(8,128)(2,1)S(1)}, u32[]{:S(2)}, u32[]{:S(2)}) %collective-permute-start.11) | collective-permute-done | bytes 1048608 | tf_op jit(solution)/shard_map/ppermute | solution.py:522
  215.9 2.1 renew.1
  (24 shorter events, 0.6 us)
Async XLA Ops:
  2.8 44.3 %copy-start.2 = (bf16[32,128,128]{2,1,0:T(8,128)(2,1)}, bf16[32,128,128]{2,1,0:T(8,128)(2,1)S(1)}, u32[]{:S(2)}) copy-start(bf16[32,128,128]{2,1,0:T(8,128)(2,1)S(1)} %get-tuple-element.25.x_ref) | copy-start | bytes 3145732
  53.4 6.3 %copy-start.1 = (bf16[4096,128]{1,0:T(8,128)(2,1)S(1)}, bf16[4096,128]{1,0:T(8,128)(2,1)}, u32[]{:S(2)}) copy-start(bf16[4096,128]{1,0:T(8,128)(2,1)} %param.10) | copy-start | bytes 3145732
  53.4 6.4 %copy-start.4 = (s32[256]{0:T(256)S(1)}, s32[256]{0:T(256)}, u32[]{:S(2)}) copy-start(s32[256]{0:T(256)} %row_ref.2) | copy-start | bytes 3076
  53.4 6.4 %copy-start.5 = (s32[256]{0:T(256)S(1)}, s32[256]{0:T(256)}, u32[]{:S(2)}) copy-start(s32[256]{0:T(256)} %col_ref.1) | copy-start | bytes 3076
  53.4 57.6 %all-to-all-start.1 = ((bf16[64,128,128]{2,1,0:T(8,128)(2,1)}), bf16[64,128,128]{2,1,0:T(8,128)(2,1)S(1)}, u32[]{:S(2)}, u32[]{:S(2)}) async-start(bf16[64,128,128]{2,1,0:T(8,128)(2,1)} %pick_rows.1), calls=%async_computation.1 | async-start | bytes 4194304 | tf_op jit(solution)/shard_map/all_to_all | solution.py:489
  59.7 3.4 %copy-start = (bf16[256,128,128]{2,1,0:T(8,128)(2,1)S(1)}, bf16[256,128,128]{2,1,0:T(8,128)(2,1)}, u32[]{:S(2)}) copy-start(bf16[256,128,128]{2,1,0:T(8,128)(2,1)} %w_ref.1) | copy-start | bytes 25165828
  63.1 1.2 copy-start.3
  64.3 46.6 %copy-start.6 = (s32[64]{0:T(128)S(1)}, s32[64]{0:T(128)}, u32[]{:S(2)}) copy-start(s32[64]{0:T(128)} %row_ref.3) | copy-start | bytes 772
  114.0 8.8 %collective-permute-start = (bf16[8,128,128]{2,1,0:T(8,128)(2,1)S(1)}, bf16[8,128,128]{2,1,0:T(8,128)(2,1)S(1)}, u32[]{:S(2)}, u32[]{:S(2)}) collective-permute-start(bf16[8,128,128]{2,1,0:T(8,128)(2,1)S(1)} %get-tuple-element.29), channel_id=1, source_target_pairs={{0,1},{1,2},{2,3},{3,0},{4,5},{5,6},{6,7},{7,4},{8,9},{9,10},{10,1... | collective-permute-start | bytes 786440 | tf_op jit(solution)/shard_map/ppermute | solution.py:499
  115.3 14.1 %collective-permute-start.1 = (bf16[8,128,128]{2,1,0:T(8,128)(2,1)S(1)}, bf16[8,128,128]{2,1,0:T(8,128)(2,1)S(1)}, u32[]{:S(2)}, u32[]{:S(2)}) collective-permute-start(bf16[8,128,128]{2,1,0:T(8,128)(2,1)S(1)} %get-tuple-element.30), channel_id=1, source_target_pairs={{0,2},{1,3},{2,0},{3,1},{4,6},{5,7},{6,4},{7,5},{8,10},{9,11},{10,... | collective-permute-start | bytes 786440 | tf_op jit(solution)/shard_map/ppermute | solution.py:499
  117.7 11.6 %collective-permute-start.2 = (bf16[8,128,128]{2,1,0:T(8,128)(2,1)S(1)}, bf16[8,128,128]{2,1,0:T(8,128)(2,1)S(1)}, u32[]{:S(2)}, u32[]{:S(2)}) collective-permute-start(bf16[8,128,128]{2,1,0:T(8,128)(2,1)S(1)} %get-tuple-element.31), channel_id=1, source_target_pairs={{0,3},{1,0},{2,1},{3,2},{4,7},{5,4},{6,5},{7,6},{8,11},{9,8},{10,9... | collective-permute-start | bytes 786440 | tf_op jit(solution)/shard_map/ppermute | solution.py:499
  130.2 5.8 %collective-permute-start.3 = (f32[320,128]{1,0:T(8,128)S(1)}, f32[320,128]{1,0:T(8,128)S(1)}, u32[]{:S(2)}, u32[]{:S(2)}) collective-permute-start(f32[320,128]{1,0:T(8,128)S(1)} %get-tuple-element.33), channel_id=1, source_target_pairs={{0,2},{1,3},{2,0},{3,1},{4,6},{5,7},{6,4},{7,5},{8,10},{9,11},{10,... | collective-permute-start | bytes 491528 | tf_op jit(solution)/shard_map/ppermute | solution.py:504
  132.4 8.0 %collective-permute-start.4 = (f32[320,128]{1,0:T(8,128)S(1)}, f32[320,128]{1,0:T(8,128)S(1)}, u32[]{:S(2)}, u32[]{:S(2)}) collective-permute-start(f32[320,128]{1,0:T(8,128)S(1)} %get-tuple-element.34), channel_id=1, source_target_pairs={{0,1},{1,2},{2,3},{3,0},{4,5},{5,6},{6,7},{7,4},{8,9},{9,10},{10,1... | collective-permute-start | bytes 491528 | tf_op jit(solution)/shard_map/ppermute | solution.py:504
  133.6 7.3 %collective-permute-start.5 = (f32[320,128]{1,0:T(8,128)S(1)}, f32[320,128]{1,0:T(8,128)S(1)}, u32[]{:S(2)}, u32[]{:S(2)}) collective-permute-start(f32[320,128]{1,0:T(8,128)S(1)} %get-tuple-element.35), channel_id=1, source_target_pairs={{0,3},{1,0},{2,1},{3,2},{4,7},{5,4},{6,5},{7,6},{8,11},{9,8},{10,9... | collective-permute-start | bytes 491528 | tf_op jit(solution)/shard_map/ppermute | solution.py:504
  141.0 36.1 %collective-permute-start.7 = (bf16[4096,128]{1,0:T(8,128)(2,1)S(1)}, bf16[4096,128]{1,0:T(8,128)(2,1)S(1)}, u32[]{:S(2)}, u32[]{:S(2)}) collective-permute-start(bf16[4096,128]{1,0:T(8,128)(2,1)S(1)} %bitcast.17), channel_id=1, source_target_pairs={{0,3},{1,0},{2,1},{3,2},{4,7},{5,4},{6,5},{7,6},{8,11},{9,8},{10,9... | collective-permute-start | bytes 3145736 | tf_op jit(solution)/shard_map/ppermute | solution.py:509
  143.6 33.4 %collective-permute-start.6 = (bf16[4096,128]{1,0:T(8,128)(2,1)S(1)}, bf16[4096,128]{1,0:T(8,128)(2,1)S(1)}, u32[]{:S(2)}, u32[]{:S(2)}) collective-permute-start(bf16[4096,128]{1,0:T(8,128)(2,1)S(1)} %bitcast.18), channel_id=1, source_target_pairs={{0,1},{1,2},{2,3},{3,0},{4,5},{5,6},{6,7},{7,4},{8,9},{9,10},{10,1... | collective-permute-start | bytes 3145736 | tf_op jit(solution)/shard_map/ppermute | solution.py:509
  177.1 9.5 %collective-permute-start.10 = (f32[320,128]{1,0:T(8,128)S(1)}, f32[320,128]{1,0:T(8,128)S(1)}, u32[]{:S(2)}, u32[]{:S(2)}) collective-permute-start(f32[320,128]{1,0:T(8,128)S(1)} %bitcast.21), channel_id=1, source_target_pairs={{0,3},{1,0},{2,1},{3,2},{4,7},{5,4},{6,5},{7,6},{8,11},{9,8},{10,9... | collective-permute-start | bytes 491528 | tf_op jit(solution)/shard_map/ppermute | solution.py:519
  180.0 6.7 %collective-permute-start.9 = (f32[320,128]{1,0:T(8,128)S(1)}, f32[320,128]{1,0:T(8,128)S(1)}, u32[]{:S(2)}, u32[]{:S(2)}) collective-permute-start(f32[320,128]{1,0:T(8,128)S(1)} %bitcast.22), channel_id=1, source_target_pairs={{0,2},{1,3},{2,0},{3,1},{4,6},{5,7},{6,4},{7,5},{8,10},{9,11},{10,... | collective-permute-start | bytes 491528 | tf_op jit(solution)/shard_map/ppermute | solution.py:519
  180.0 10.5 %collective-permute-start.8 = (f32[320,128]{1,0:T(8,128)S(1)}, f32[320,128]{1,0:T(8,128)S(1)}, u32[]{:S(2)}, u32[]{:S(2)}) collective-permute-start(f32[320,128]{1,0:T(8,128)S(1)} %bitcast.23), channel_id=1, source_target_pairs={{0,1},{1,2},{2,3},{3,0},{4,5},{5,6},{6,7},{7,4},{8,9},{9,10},{10,1... | collective-permute-start | bytes 491528 | tf_op jit(solution)/shard_map/ppermute | solution.py:519
  190.5 25.4 %collective-permute-start.11 = (bf16[4096,128]{1,0:T(8,128)(2,1)S(1)}, bf16[4096,128]{1,0:T(8,128)(2,1)S(1)}, u32[]{:S(2)}, u32[]{:S(2)}) collective-permute-start(bf16[4096,128]{1,0:T(8,128)(2,1)S(1)} %bitcast.19), channel_id=1, source_target_pairs={{0,2},{1,3},{2,0},{3,1},{4,6},{5,7},{6,4},{7,5},{8,10},{9,11},{10,... | collective-permute-start | bytes 3145736 | tf_op jit(solution)/shard_map/ppermute | solution.py:522

commit v4 on v3

--- a/solution.py
+++ b/solution.py
@@ -192,7 +192,8 @@
 
 
 def far_kernel(own_ref, row_ref, w_hbm, acc_hbm, arrived_ref, *rest):
-    whole_ref, part_refs, (far_ref, acc_ref, w_ref, x_ref, sems) = rest[0], rest[1:-5], rest[-5:]
+    whole_ref, half_refs, part_refs = rest[0], rest[1:3], rest[3:-5]
+    far_ref, acc_ref, w_ref, x_ref, sems = rest[-5:]
     count = w_ref.shape[0]
     units = arrived_ref.shape[0]
     groups = count // 16
@@ -220,13 +221,14 @@
             row = row_ref[block]
             far_ref[row] += jnp.dot(w_ref[block], x_ref[block], preferred_element_type=jnp.float32)
     acc_copy.wait()
+    whole_ref[...] = (time_step * (acc_ref[...] + far_ref[...])).astype(jnp.bfloat16)
+    half_rows = half_refs[0].shape[0]
+    for h in range(2):
+        half_refs[h][...] = whole_ref[h * half_rows : (h + 1) * half_rows]
     parts = len(part_refs)
     for k in range(parts):
         share = part_refs[k].shape[0]
-        here = pl.ds(lax.rem(own_ref[0] + k, parts) * share, share)
-        stepped = (time_step * (acc_ref[here] + far_ref[here])).astype(jnp.bfloat16)
-        part_refs[k][...] = stepped
-        whole_ref[here] = stepped
+        part_refs[k][...] = whole_ref[pl.ds(lax.rem(own_ref[0] + k, parts) * share, share)]
 
 
 def far_product(own, remote_row, remote_w, acc, arrived, parts):
@@ -238,8 +240,9 @@
     return pl.pallas_call(
         far_kernel,
         in_specs=[smem, smem, hbm, hbm, vmem],
-        out_specs=[vmem] * (1 + parts),
+        out_specs=[vmem] * (3 + parts),
         out_shape=[jax.ShapeDtypeStruct((block_rows, side, width), jnp.bfloat16)]
+        + [jax.ShapeDtypeStruct((block_rows // 2, side, width), jnp.bfloat16)] * 2
         + [jax.ShapeDtypeStruct((block_rows // parts, side, width), jnp.bfloat16)] * parts,
         scratch_shapes=[
             pltpu.VMEM((block_rows, side, width), jnp.float32),
@@ -326,7 +329,12 @@
             for p in range(q):
                 own = own - lower[q][p] * rows[p]
             rows.append(own)
-        for t in range(t0 + 1, tiles):
+        done, pivots = rows[0], splat[0][0]
+        for q in range(1, 8):
+            done = jnp.where(sub == q, rows[q], done)
+            pivots = jnp.where(sub == q, splat[q][q], pivots)
+        done = done * lax.rsqrt(pivots)
+        for t in range(t0 + 1, min(t0 + 3, tiles)):
             reduced = []
             fresh = jnp.where(in_panel, 0.0, v[t])
             for p in range(8):
@@ -336,11 +344,11 @@
                 reduced.append(mine)
                 fresh = fresh - (mine * recip[p]) * rows[p]
             v[t] = fresh
-        done, pivots = rows[0], splat[0][0]
-        for q in range(1, 8):
-            done = jnp.where(sub == q, rows[q], done)
-            pivots = jnp.where(sub == q, splat[q][q], pivots)
-        inverse.append(jnp.where(lane <= sub + base, done * lax.rsqrt(pivots), 0.0))
+        if t0 + 3 < tiles:
+            change = split_dot(done, done, 0, 0)
+            for t in range(t0 + 3, tiles):
+                v[t] = jnp.where(in_panel, 0.0, v[t]) - change[8 * t : 8 * t + 8, :]
+        inverse.append(jnp.where(lane <= sub + base, done, 0.0))
         log_row = log_row + jnp.where(lane == sub + base, 0.5 * jnp.log(pivots), 0.0)
     return jnp.concatenate(inverse, axis=0), jnp.sum(log_row, axis=0, keepdims=True)
 
@@ -365,26 +373,18 @@
         m_ref[low, low + 2, pl.ds(pl.multiple_of(device // 2 * half, half), half), :] = (
             refs[k][2 * side :, :] * scale
         )
-    sub = lax.broadcasted_iota(jnp.int32, (side, side), 0)
-    lane = lax.broadcasted_iota(jnp.int32, (side, side), 1)
-    eye = (sub == lane).astype(jnp.float32)
-
-    @pl.loop(0, parts)
-    def _(k):
+    for k in range(parts):
         inverse, logs = factor_block(m_ref[k, k])
-        log_ref[pl.ds(k, 1), :] = logs
+        log_ref[k : k + 1, :] = logs
         for b in range(parts):
-            block = jnp.where(k == b, eye, m_ref[k, b])
-            z_ref[b] = split_dot(inverse, block, 1, 0)
+            z_ref[b] = inverse if b == k else split_dot(inverse, m_ref[k, b], 1, 0)
         for b in range(parts):
-            inv_ref[k, b] = jnp.where(b <= k, z_ref[b], 0.0).astype(jnp.bfloat16)
-        for a in range(1, parts):
-
-            @pl.when(a > k)
-            def _():
-                for b in range(parts):
+            inv_ref[k, b] = (z_ref[b] if b <= k else jnp.zeros((side, side))).astype(jnp.bfloat16)
+        for a in range(k + 1, parts):
+            for b in range(parts):
+                if b <= k or b >= a:
                     change = split_dot(z_ref[a], z_ref[b], 0, 0)
-                    m_ref[a, b] = jnp.where(k == b, 0.0, m_ref[a, b]) - change
+                    m_ref[a, b] = -change if b == k else m_ref[a, b] - change
 
 
 def cholesky_parts(own, quarters, unit_total):
@@ -411,10 +411,9 @@
     )(own, *quarters)
 
 
-def renew_kernel(own_ref, *refs):
-    x_refs, (inv_ref, out_hbm, out_ref, sems) = refs[:-4], refs[-4:]
+def renew_kernel(own_ref, own_rows, back1, near2, far2, back3, inv_ref, out_hbm, out_ref, sems):
     own = own_ref[0]
-    parts = len(x_refs)
+    parts = inv_ref.shape[0]
     chunks = sems.shape[0]
     chunk = out_ref.shape[0] // chunks
     inverse = jnp.concatenate(
@@ -423,7 +422,9 @@
     copies = []
     for c in range(chunks):
         here = pl.ds(c * chunk, chunk)
-        vectors = jnp.concatenate([x_ref[here, :] for x_ref in x_refs], axis=1)
+        back2 = (near2, far2)[c // (chunks // 2)]
+        rows2 = back2[pl.ds(c % (chunks // 2) * chunk, chunk), :]
+        vectors = jnp.concatenate([own_rows[here, :], back1[here, :], rows2, back3[here, :]], axis=1)
         out_ref[here, :] = lax.dot_general(
             vectors, inverse, (((1,), (1,)), ((), ())), preferred_element_type=jnp.float32
         ).astype(jnp.bfloat16)
@@ -434,13 +435,12 @@
 
 
 def renew(own, vectors, inverse):
-    parts = len(vectors)
     rows, width = vectors[0].shape
-    side = inverse.shape[-1]
+    parts, _, side, _ = inverse.shape
     vmem = pl.BlockSpec(memory_space=pltpu.VMEM)
     return pl.pallas_call(
         renew_kernel,
-        in_specs=[pl.BlockSpec(memory_space=pltpu.SMEM)] + [vmem] * (parts + 1),
+        in_specs=[pl.BlockSpec(memory_space=pltpu.SMEM)] + [vmem] * (len(vectors) + 1),
         out_specs=pl.BlockSpec(memory_space=pltpu.HBM),
         out_shape=pltpu.HBM((rows, side), jnp.bfloat16),
         scratch_shapes=[
@@ -492,7 +492,7 @@
     steps = (2, 1, 3)
     assert parts == 4
     acc = local_product(local_row, local_col, local_w, pieces, blocks)
-    stepped, *outgoing = far_product(own, remote_row, remote_w, acc, arrived, parts)
+    stepped, near, far, *outgoing = far_product(own, remote_row, remote_w, acc, arrived, parts)
 
     row_parts = [outgoing[0]] + [None] * 3
     for k in steps:
@@ -503,24 +503,25 @@
     for k in steps:
         mine = mine + lax.ppermute(quarters[k], "vec", around(parts, k))
 
-    late, mine = lax.optimization_barrier((stepped.reshape(rows_dev, width), mine))
-    vectors = [late] + [None] * 3
-    for k in (1, 3):
-        vectors[k] = lax.ppermute(late, "vec", around(parts, k))
+    stepped, mine = lax.optimization_barrier((stepped, mine))
+    back1, back3 = (lax.ppermute(stepped, "vec", around(parts, k)) for k in (1, 3))
 
     share = mine.size // units
     by_unit = lax.all_to_all(mine.reshape(units, 1, share), "unit", 0, 0, tiled=True)
     summed = jnp.sum(by_unit, axis=0, keepdims=True)
+    near, summed = lax.optimization_barrier((near, summed))
+    near2 = lax.ppermute(near, "vec", around(parts, 2))
     spread_sum = jnp.broadcast_to(summed, (units, 1, share))
     quarter = lax.all_to_all(spread_sum, "unit", 0, 0, tiled=True).reshape(mine.shape)
-    quarter, vectors[1], vectors[3] = lax.optimization_barrier((quarter, vectors[1], vectors[3]))
+    quarter, back1, back3, near2 = lax.optimization_barrier((quarter, back1, back3, near2))
     gathered = [quarter] + [None] * 3
     for k in steps:
         gathered[k] = lax.ppermute(quarter, "vec", around(parts, k))
 
-    later, gathered = lax.optimization_barrier((late, gathered))
-    vectors[2] = lax.ppermute(later, "vec", around(parts, 2))
+    far, gathered = lax.optimization_barrier((far, gathered))
+    far2 = lax.ppermute(far, "vec", around(parts, 2))
     inverse, logs = cholesky_parts(own, gathered, unit_total)
+    vectors = [rows.reshape(-1, width) for rows in (stepped, back1, near2, far2, back3)]
     renewed = renew(own, vectors, inverse)
     return (renewed, logs.reshape(parts * width))
 

time: 219 us -> 217 us (level)
  waiting for transfers between devices: 65.6 us -> 62 us
    ppermute x3 -> x4, starting transfers between devices: 3.26 us -> 5.07 us  [the longest x2 2.68 us: body(): lax.ppermute(stepped, 'vec', around(parts, k))]
    unnamed x14 -> x18, local copies, waits for them, and re-layouts: 4.62 us -> 4.63 us
  transfers between devices with their start and end apart: 13 -> 14, of which waited for: 10 -> 10; matrix products, arithmetic and copies ran while one was open for 0% -> 0% of each run, Pallas kernels for 15% -> 14%
where the time goes in v4:
time: 217 us; the launch traced here: 216 us
  blocking collectives  77.8 us (36%)
  waiting for transfers between devices  62 us (29%)
  Pallas kernels  45.4 us (21%)
  starting transfers between devices  25 us (12%)
  local copies, waits for them, and re-layouts  4.8 us (2%)
    all_to_all x1, blocking collectives, body(): table = lax.all_to_all(spread, 'unit', 0, 0, tiled=True)  44.3 us
    all_to_all x1, waiting for transfers between devices, body(): arrived = lax.all_to_all(chosen, 'unit', 0, 0, tiled=True)  37 us
    pallas_call x1, Pallas kernels, cholesky_parts(): pl.pallas_call(functools.partial(factor_kernel, 1.0 / unit_total), in_spe...  20.3 us
    all_to_all x1, blocking collectives, body(): lax.all_to_all(mine.reshape(units, 1, share), 'unit', 0, 0, tiled=True)  17.4 us
    all_to_all x1, blocking collectives, body(): lax.all_to_all(spread_sum, 'unit', 0, 0, tiled=True).reshape(mine.shape)  16 us
    ppermute x3, waiting for transfers between devices, body(): row_parts[k] = lax.ppermute(outgoing[k], 'vec', around(parts, k))  10.5 us
    pallas_call x1, Pallas kernels, local_product(): pl.pallas_call(local_kernel, grid_spec=pltpu.PrefetchScalarGridSpec(num_s...  9.61 us
    ppermute x3, waiting for transfers between devices, body(): gathered[k] = lax.ppermute(quarter, 'vec', around(parts, k))  8.38 us
  transfers between devices with their start and end apart: 14, of which 10 were waited for; matrix products, arithmetic and copies ran while one was open for 0% of the time, Pallas kernels for 14%

profile of v4, /device:TPU:1, one launch (start us, length us, event | category | flops | bytes accessed | tf_op | source)
XLA Modules:
  0.0 216.2 jit_solution(2947857712812297873)
XLA Ops:
  0.6 2.1 spread_pieces.1
  2.8 44.3 %all_to_all.20.table_ref = bf16[64,72,128]{2,1,0:T(8,128)(2,1)S(1)} all-to-all(bf16[64,72,128]{2,1,0:T(8,128)(2,1)S(1)} %get-tuple-element.31), channel_id=1, replica_groups=mesh['unit'=64,'vec'=4] {'unit'}, dimensions={0} | all-to-all | bytes 2359296 | tf_op jit(solution)/shard_map/all_to_all | solution.py:485
  47.3 6.1 %pick_rows.1 = bf16[64,128,128]{2,1,0:T(8,128)(2,1)} custom-call(f32[4,8,128]{2,1,0:T(8,128)S(1)} %reshape.73.index_ref, bf16[64,72,128]{2,1,0:T(8,128)(2,1)S(1)} %all_to_all.20.table_ref), custom_call_target="tpu_custom_call" | custom-call | flops 4000000000 | bytes 4194304 | tf_op jit(solution)/shard_map/pick_rows/pallas_call | solution.py:177
  53.4 6.3 %all-to-all-start.1 = ((bf16[64,128,128]{2,1,0:T(8,128)(2,1)}), bf16[64,128,128]{2,1,0:T(8,128)(2,1)S(1)}, u32[]{:S(2)}, u32[]{:S(2)}) async-start(bf16[64,128,128]{2,1,0:T(8,128)(2,1)} %pick_rows.1), calls=%async_computation.1 | async-start | bytes 4194304 | tf_op jit(solution)/shard_map/all_to_all | solution.py:489
  59.7 3.4 %copy-done = bf16[256,128,128]{2,1,0:T(8,128)(2,1)S(1)} copy-done((bf16[256,128,128]{2,1,0:T(8,128)(2,1)S(1)}, bf16[256,128,128]{2,1,0:T(8,128)(2,1)}, u32[]{:S(2)}) %copy-start) | copy-done | bytes 8388632
  63.1 1.2 copy-done.3
  64.3 9.6 %local_blocks.1.acc_hbm = f32[32,128,128]{2,1,0:T(8,128)} custom-call(s32[256]{0:T(256)S(1)} %copy-done.4, s32[256]{0:T(256)S(1)} %copy-done.5, bf16[256,128,128]{2,1,0:T(8,128)(2,1)S(1)} %copy-done, bf16[32,128,128]{2,1,0:T(8,128)(2,1)S(1)} %copy-done.3, bf16[32,128,128]{2,1,0:T(8,128)(2,1)S(1)} %bitcast.20), custom_call_target="tpu_custom_call" | custom-call | flops 1073741824 | bytes 14680064 | tf_op jit(solution)/shard_map/local_blocks/pallas_call | solution.py:47
  73.9 37.0 %all-to-all-done.1.arrived_ref = bf16[64,128,128]{2,1,0:T(8,128)(2,1)S(1)} async-done(((bf16[64,128,128]{2,1,0:T(8,128)(2,1)}), bf16[64,128,128]{2,1,0:T(8,128)(2,1)S(1)}, u32[]{:S(2)}, u32[]{:S(2)}) %all-to-all-start.1) | async-done | bytes 2097184 | tf_op jit(solution)/shard_map/all_to_all | solution.py:489
  110.9 3.3 %far_blocks.1 = (bf16[32,128,128]{2,1,0:T(8,128)(2,1)S(1)}, bf16[16,128,128]{2,1,0:T(8,128)(2,1)S(1)}, bf16[16,128,128]{2,1,0:T(8,128)(2,1)S(1)}, bf16[8,128,128...) custom-call(s32[1]{0:T(128)} %bitcast.own_ref, ...), custom_call_target="tpu_custom_call" | custom-call | flops 268435456 | bytes 8388608 | tf_op jit(solution)/shard_map/far_blocks/pallas_call | solution.py:240
  114.3 1.3 collective-permute-start
  115.5 2.5 %collective-permute-start.1 = (bf16[8,128,128]{2,1,0:T(8,128)(2,1)S(1)}, bf16[8,128,128]{2,1,0:T(8,128)(2,1)S(1)}, u32[]{:S(2)}, u32[]{:S(2)}) collective-permute-start(bf16[8,128,128]{2,1,0:T(8,128)(2,1)S(1)} %get-tuple-element.35), channel_id=1, source_target_pairs={{0,2},{1,3},{2,0},{3,1},{4,6},{5,7},{6,4},{7,5},{8,10},{9,11},{10,... | collective-permute-start | bytes 786440 | tf_op jit(solution)/shard_map/ppermute | solution.py:499
  118.0 1.1 collective-permute-start.2
  119.1 3.9 %collective-permute-done = bf16[8,128,128]{2,1,0:T(8,128)(2,1)S(1)} collective-permute-done((bf16[8,128,128]{2,1,0:T(8,128)(2,1)S(1)}, bf16[8,128,128]{2,1,0:T(8,128)(2,1)S(1)}, u32[]{:S(2)}, u32[]{:S(2)}) %collective-permute-start) | collective-permute-done | bytes 262176 | tf_op jit(solution)/shard_map/ppermute | solution.py:499
  123.0 6.6 %collective-permute-done.1 = bf16[8,128,128]{2,1,0:T(8,128)(2,1)S(1)} collective-permute-done((bf16[8,128,128]{2,1,0:T(8,128)(2,1)S(1)}, bf16[8,128,128]{2,1,0:T(8,128)(2,1)S(1)}, u32[]{:S(2)}, u32[]{:S(2)}) %collective-permute-start.1) | collective-permute-done | bytes 262176 | tf_op jit(solution)/shard_map/ppermute | solution.py:499
  129.6 0.8 gram_quarters.1
  130.5 2.2 %collective-permute-start.3 = (f32[320,128]{1,0:T(8,128)S(1)}, f32[320,128]{1,0:T(8,128)S(1)}, u32[]{:S(2)}, u32[]{:S(2)}) collective-permute-start(f32[320,128]{1,0:T(8,128)S(1)} %get-tuple-element.38), channel_id=1, source_target_pairs={{0,2},{1,3},{2,0},{3,1},{4,6},{5,7},{6,4},{7,5},{8,10},{9,11},{10,... | collective-permute-start | bytes 491528 | tf_op jit(solution)/shard_map/ppermute | solution.py:504
  132.6 1.2 collective-permute-start.4
  133.8 1.5 collective-permute-start.5
  135.3 1.2 collective-permute-done.3
  136.5 4.1 %collective-permute-done.4 = f32[320,128]{1,0:T(8,128)S(1)} collective-permute-done((f32[320,128]{1,0:T(8,128)S(1)}, f32[320,128]{1,0:T(8,128)S(1)}, u32[]{:S(2)}, u32[]{:S(2)}) %collective-permute-start.4) | collective-permute-done | bytes 163872 | tf_op jit(solution)/shard_map/ppermute | solution.py:504
  141.2 2.7 %collective-permute-start.7 = (bf16[32,128,128]{2,1,0:T(8,128)(2,1)S(1)}, bf16[32,128,128]{2,1,0:T(8,128)(2,1)S(1)}, u32[]{:S(2)}, u32[]{:S(2)}) collective-permute-start(bf16[32,128,128]{2,1,0:T(8,128)(2,1)S(1)} %get-tuple-element.41), channel_id=1, source_target_pairs={{0,3},{1,0},{2,1},{3,2},{4,7},{5,4},{6,5},{7,6},{8,11},{9,8},{10,9... | collective-permute-start | bytes 3145736 | tf_op jit(solution)/shard_map/ppermute | solution.py:507
  143.9 17.4 %all_to_all.21 = f32[64,1,640]{2,1,0:T(1,128)S(1)} all-to-all(f32[64,1,640]{2,1,0:T(1,128)S(1)} %bitcast.33), channel_id=1, replica_groups=mesh['unit'=64,'vec'=4] {'unit'}, dimensions={0} | all-to-all | bytes 327680 | tf_op jit(solution)/shard_map/all_to_all | solution.py:510
  161.5 1.4 collective-permute-start.8
  163.0 16.0 %all_to_all.22 = f32[64,1,640]{2,1,0:T(1,128)S(1)} all-to-all(f32[64,1,640]{2,1,0:T(1,128)S(1)} %broadcast_in_dim.12), channel_id=1, replica_groups=mesh['unit'=64,'vec'=4] {'unit'}, dimensions={0} | all-to-all | bytes 327680 | tf_op jit(solution)/shard_map/all_to_all | solution.py:515
  179.2 1.6 collective-permute-start.11
  180.8 2.3 %collective-permute-start.10 = (f32[320,128]{1,0:T(8,128)S(1)}, f32[320,128]{1,0:T(8,128)S(1)}, u32[]{:S(2)}, u32[]{:S(2)}) collective-permute-start(f32[320,128]{1,0:T(8,128)S(1)} %bitcast.26), channel_id=1, source_target_pairs={{0,2},{1,3},{2,0},{3,1},{4,6},{5,7},{6,4},{7,5},{8,10},{9,11},{10,... | collective-permute-start | bytes 491528 | tf_op jit(solution)/shard_map/ppermute | solution.py:519
  183.1 0.9 collective-permute-done.11.refs_3_
  184.0 2.5 %collective-permute-done.10.refs_2_ = f32[320,128]{1,0:T(8,128)S(1)} collective-permute-done((f32[320,128]{1,0:T(8,128)S(1)}, f32[320,128]{1,0:T(8,128)S(1)}, u32[]{:S(2)}, u32[]{:S(2)}) %collective-permute-start.10) | collective-permute-done | bytes 163872 | tf_op jit(solution)/shard_map/ppermute | solution.py:519
  186.5 5.0 %collective-permute-done.9.refs_1_ = f32[320,128]{1,0:T(8,128)S(1)} collective-permute-done((f32[320,128]{1,0:T(8,128)S(1)}, f32[320,128]{1,0:T(8,128)S(1)}, u32[]{:S(2)}, u32[]{:S(2)}) %collective-permute-start.9) | collective-permute-done | bytes 163872 | tf_op jit(solution)/shard_map/ppermute | solution.py:519
  191.5 1.0 collective-permute-start.12
  192.5 20.3 %factor.1 = (bf16[4,4,128,128]{3,2,1,0:T(8,128)(2,1)S(1)}, f32[4,128]{1,0:T(4,128)}) custom-call(s32[1]{0:T(128)} %bitcast.own_ref, f32[320,128]{1,0:T(8,128)S(1)} %bitcast.28, f32[320,128]{1,0:T(8,128)S(1)} %collective-permute-done.9.refs_1_, f32[320,128]{1,0:T(8,128)S(1)} %collective-permute-done.10.refs_2_, f32[320,128]{1,0:T(8,128)S(1)} %collective-permute-done.11.refs_3_), custom_call_target="tpu_custom_call" | custom-call | flops 200000000 | bytes 2097152 | tf_op jit(solution)/shard_map/factor/pallas_call | solution.py:394
  212.9 3.2 %renew.1 = bf16[4096,128]{1,0:T(8,128)(2,1)} custom-call(s32[1]{0:T(128)} %bitcast.own_ref, bf16[4096,128]{1,0:T(8,128)(2,1)S(1)} %bitcast.21, bf16[4096,128]{1,0:T(8,128)(2,1)S(1)} %bitcast.23, bf16[2048,128]{1,0:T(8,128)(2,1)} %bitcast.15.near2, bf16[2048,128]{1,0:T(8,128)(2,1)S(1)} %bitcast.24, bf16[4096,128]{1,0:T(8,128)(2,1)S(1)} %bitcast.22, ...), custom_call_target="tpu_custom_call" | custom-call | flops 536870912 | bytes 6291456 | tf_op jit(solution)/shard_map/renew/pallas_call | solution.py:441
  (32 shorter events, 1.3 us)
Async XLA Ops:
  2.8 44.3 %copy-start.2 = (bf16[32,128,128]{2,1,0:T(8,128)(2,1)}, bf16[32,128,128]{2,1,0:T(8,128)(2,1)S(1)}, u32[]{:S(2)}) copy-start(bf16[32,128,128]{2,1,0:T(8,128)(2,1)S(1)} %get-tuple-element.30.x_ref) | copy-start | bytes 3145732
  53.4 6.3 %copy-start.1 = (bf16[4096,128]{1,0:T(8,128)(2,1)S(1)}, bf16[4096,128]{1,0:T(8,128)(2,1)}, u32[]{:S(2)}) copy-start(bf16[4096,128]{1,0:T(8,128)(2,1)} %param.10) | copy-start | bytes 3145732
  53.4 6.4 %copy-start.4 = (s32[256]{0:T(256)S(1)}, s32[256]{0:T(256)}, u32[]{:S(2)}) copy-start(s32[256]{0:T(256)} %row_ref.2) | copy-start | bytes 3076
  53.4 6.4 %copy-start.5 = (s32[256]{0:T(256)S(1)}, s32[256]{0:T(256)}, u32[]{:S(2)}) copy-start(s32[256]{0:T(256)} %col_ref.1) | copy-start | bytes 3076
  53.4 57.6 %all-to-all-start.1 = ((bf16[64,128,128]{2,1,0:T(8,128)(2,1)}), bf16[64,128,128]{2,1,0:T(8,128)(2,1)S(1)}, u32[]{:S(2)}, u32[]{:S(2)}) async-start(bf16[64,128,128]{2,1,0:T(8,128)(2,1)} %pick_rows.1), calls=%async_computation.1 | async-start | bytes 4194304 | tf_op jit(solution)/shard_map/all_to_all | solution.py:489
  59.7 3.4 %copy-start = (bf16[256,128,128]{2,1,0:T(8,128)(2,1)S(1)}, bf16[256,128,128]{2,1,0:T(8,128)(2,1)}, u32[]{:S(2)}) copy-start(bf16[256,128,128]{2,1,0:T(8,128)(2,1)} %w_ref.1) | copy-start | bytes 25165828
  63.1 1.2 copy-start.3
  64.3 46.6 %copy-start.6 = (s32[64]{0:T(128)S(1)}, s32[64]{0:T(128)}, u32[]{:S(2)}) copy-start(s32[64]{0:T(128)} %row_ref.3) | copy-start | bytes 772
  114.2 27.0 %copy-start.7 = (bf16[16,128,128]{2,1,0:T(8,128)(2,1)}, bf16[16,128,128]{2,1,0:T(8,128)(2,1)S(1)}, u32[]{:S(2)}) copy-start(bf16[16,128,128]{2,1,0:T(8,128)(2,1)S(1)} %get-tuple-element.50) | copy-start | bytes 1572868
  114.2 29.7 %copy-start.8 = (bf16[16,128,128]{2,1,0:T(8,128)(2,1)}, bf16[16,128,128]{2,1,0:T(8,128)(2,1)S(1)}, u32[]{:S(2)}) copy-start(bf16[16,128,128]{2,1,0:T(8,128)(2,1)S(1)} %get-tuple-element.45) | copy-start | bytes 1572868
  114.3 8.8 %collective-permute-start = (bf16[8,128,128]{2,1,0:T(8,128)(2,1)S(1)}, bf16[8,128,128]{2,1,0:T(8,128)(2,1)S(1)}, u32[]{:S(2)}, u32[]{:S(2)}) collective-permute-start(bf16[8,128,128]{2,1,0:T(8,128)(2,1)S(1)} %get-tuple-element.34), channel_id=1, source_target_pairs={{0,1},{1,2},{2,3},{3,0},{4,5},{5,6},{6,7},{7,4},{8,9},{9,10},{10,1... | collective-permute-start | bytes 786440 | tf_op jit(solution)/shard_map/ppermute | solution.py:499
  115.5 14.1 %collective-permute-start.1 = (bf16[8,128,128]{2,1,0:T(8,128)(2,1)S(1)}, bf16[8,128,128]{2,1,0:T(8,128)(2,1)S(1)}, u32[]{:S(2)}, u32[]{:S(2)}) collective-permute-start(bf16[8,128,128]{2,1,0:T(8,128)(2,1)S(1)} %get-tuple-element.35), channel_id=1, source_target_pairs={{0,2},{1,3},{2,0},{3,1},{4,6},{5,7},{6,4},{7,5},{8,10},{9,11},{10,... | collective-permute-start | bytes 786440 | tf_op jit(solution)/shard_map/ppermute | solution.py:499
  118.0 11.7 %collective-permute-start.2 = (bf16[8,128,128]{2,1,0:T(8,128)(2,1)S(1)}, bf16[8,128,128]{2,1,0:T(8,128)(2,1)S(1)}, u32[]{:S(2)}, u32[]{:S(2)}) collective-permute-start(bf16[8,128,128]{2,1,0:T(8,128)(2,1)S(1)} %get-tuple-element.36), channel_id=1, source_target_pairs={{0,3},{1,0},{2,1},{3,2},{4,7},{5,4},{6,5},{7,6},{8,11},{9,8},{10,9... | collective-permute-start | bytes 786440 | tf_op jit(solution)/shard_map/ppermute | solution.py:499
  130.5 6.1 %collective-permute-start.3 = (f32[320,128]{1,0:T(8,128)S(1)}, f32[320,128]{1,0:T(8,128)S(1)}, u32[]{:S(2)}, u32[]{:S(2)}) collective-permute-start(f32[320,128]{1,0:T(8,128)S(1)} %get-tuple-element.38), channel_id=1, source_target_pairs={{0,2},{1,3},{2,0},{3,1},{4,6},{5,7},{6,4},{7,5},{8,10},{9,11},{10,... | collective-permute-start | bytes 491528 | tf_op jit(solution)/shard_map/ppermute | solution.py:504
  132.6 8.0 %collective-permute-start.4 = (f32[320,128]{1,0:T(8,128)S(1)}, f32[320,128]{1,0:T(8,128)S(1)}, u32[]{:S(2)}, u32[]{:S(2)}) collective-permute-start(f32[320,128]{1,0:T(8,128)S(1)} %get-tuple-element.39), channel_id=1, source_target_pairs={{0,1},{1,2},{2,3},{3,0},{4,5},{5,6},{6,7},{7,4},{8,9},{9,10},{10,1... | collective-permute-start | bytes 491528 | tf_op jit(solution)/shard_map/ppermute | solution.py:504
  133.8 7.3 %collective-permute-start.5 = (f32[320,128]{1,0:T(8,128)S(1)}, f32[320,128]{1,0:T(8,128)S(1)}, u32[]{:S(2)}, u32[]{:S(2)}) collective-permute-start(f32[320,128]{1,0:T(8,128)S(1)} %get-tuple-element.40), channel_id=1, source_target_pairs={{0,3},{1,0},{2,1},{3,2},{4,7},{5,4},{6,5},{7,6},{8,11},{9,8},{10,9... | collective-permute-start | bytes 491528 | tf_op jit(solution)/shard_map/ppermute | solution.py:504
  141.2 38.0 %collective-permute-start.7 = (bf16[32,128,128]{2,1,0:T(8,128)(2,1)S(1)}, bf16[32,128,128]{2,1,0:T(8,128)(2,1)S(1)}, u32[]{:S(2)}, u32[]{:S(2)}) collective-permute-start(bf16[32,128,128]{2,1,0:T(8,128)(2,1)S(1)} %get-tuple-element.41), channel_id=1, source_target_pairs={{0,3},{1,0},{2,1},{3,2},{4,7},{5,4},{6,5},{7,6},{8,11},{9,8},{10,9... | collective-permute-start | bytes 3145736 | tf_op jit(solution)/shard_map/ppermute | solution.py:507
  143.9 35.3 %collective-permute-start.6 = (bf16[32,128,128]{2,1,0:T(8,128)(2,1)S(1)}, bf16[32,128,128]{2,1,0:T(8,128)(2,1)S(1)}, u32[]{:S(2)}, u32[]{:S(2)}) collective-permute-start(bf16[32,128,128]{2,1,0:T(8,128)(2,1)S(1)} %get-tuple-element.41), channel_id=1, source_target_pairs={{0,1},{1,2},{2,3},{3,0},{4,5},{5,6},{6,7},{7,4},{8,9},{9,10},{10,1... | collective-permute-start | bytes 3145736 | tf_op jit(solution)/shard_map/ppermute | solution.py:507
  161.5 17.7 %collective-permute-start.8 = (bf16[16,128,128]{2,1,0:T(8,128)(2,1)}, bf16[16,128,128]{2,1,0:T(8,128)(2,1)}, u32[]{:S(2)}, u32[]{:S(2)}) collective-permute-start(bf16[16,128,128]{2,1,0:T(8,128)(2,1)} %copy-done.8), channel_id=1, source_target_pairs={{0,2},{1,3},{2,0},{3,1},{4,6},{5,7},{6,4},{7,5},{8,10},{9,11},{10,... | collective-permute-start | bytes 1572872 | tf_op jit(solution)/shard_map/ppermute | solution.py:513
  179.2 4.8 %collective-permute-start.11 = (f32[320,128]{1,0:T(8,128)S(1)}, f32[320,128]{1,0:T(8,128)S(1)}, u32[]{:S(2)}, u32[]{:S(2)}) collective-permute-start(f32[320,128]{1,0:T(8,128)S(1)} %bitcast.25), channel_id=1, source_target_pairs={{0,3},{1,0},{2,1},{3,2},{4,7},{5,4},{6,5},{7,6},{8,11},{9,8},{10,9... | collective-permute-start | bytes 491528 | tf_op jit(solution)/shard_map/ppermute | solution.py:519
  180.8 5.7 %collective-permute-start.10 = (f32[320,128]{1,0:T(8,128)S(1)}, f32[320,128]{1,0:T(8,128)S(1)}, u32[]{:S(2)}, u32[]{:S(2)}) collective-permute-start(f32[320,128]{1,0:T(8,128)S(1)} %bitcast.26), channel_id=1, source_target_pairs={{0,2},{1,3},{2,0},{3,1},{4,6},{5,7},{6,4},{7,5},{8,10},{9,11},{10,... | collective-permute-start | bytes 491528 | tf_op jit(solution)/shard_map/ppermute | solution.py:519
  183.1 8.4 %collective-permute-start.9 = (f32[320,128]{1,0:T(8,128)S(1)}, f32[320,128]{1,0:T(8,128)S(1)}, u32[]{:S(2)}, u32[]{:S(2)}) collective-permute-start(f32[320,128]{1,0:T(8,128)S(1)} %bitcast.27), channel_id=1, source_target_pairs={{0,1},{1,2},{2,3},{3,0},{4,5},{5,6},{6,7},{7,4},{8,9},{9,10},{10,1... | collective-permute-start | bytes 491528 | tf_op jit(solution)/shard_map/ppermute | solution.py:519
  191.5 21.4 %collective-permute-start.12 = (bf16[16,128,128]{2,1,0:T(8,128)(2,1)}, bf16[16,128,128]{2,1,0:T(8,128)(2,1)S(1)}, u32[]{:S(2)}, u32[]{:S(2)}) collective-permute-start(bf16[16,128,128]{2,1,0:T(8,128)(2,1)} %copy-done.7), channel_id=1, source_target_pairs={{0,2},{1,3},{2,0},{3,1},{4,6},{5,7},{6,4},{7,5},{8,10},{9,11},{10,... | collective-permute-start | bytes 1572872 | tf_op jit(solution)/shard_map/ppermute | solution.py:522

commit v5 on v4

--- a/solution.py
+++ b/solution.py
@@ -172,7 +172,7 @@
 def pick_rows(index, table, block_rows):
     units, far_count = index.shape
     width = table.shape[-1]
-    steps = 4
+    steps = 2
     lines = units * far_count // width // steps
     return pl.pallas_call(
         functools.partial(pick_kernel, block_rows),
@@ -358,9 +358,6 @@
     parts = m_ref.shape[0]
     side = m_ref.shape[2]
     half = side // 2
-    for a in range(parts):
-        for b in range(a):
-            m_ref[a, b] = jnp.zeros((side, side), jnp.float32)
     for k in range(parts):
         device = lax.rem(own_ref[0] + parts - k, parts)
         after = lax.rem(device + 1, parts)

time: 217 us -> 216 us (level)
  no operation moved by 1% of the time
where the time goes in v5:
time: 216 us
  blocking collectives  77.8 us (36%)
  waiting for transfers between devices  62 us (29%)
  Pallas kernels  45.2 us (21%)
  starting transfers between devices  24.8 us (11%)
  local copies, waits for them, and re-layouts  4.8 us (2%)
    all_to_all x1, blocking collectives, body(): table = lax.all_to_all(spread, 'unit', 0, 0, tiled=True)  44.3 us
    all_to_all x1, waiting for transfers between devices, body(): arrived = lax.all_to_all(chosen, 'unit', 0, 0, tiled=True)  37 us
    pallas_call x1, Pallas kernels, cholesky_parts(): pl.pallas_call(functools.partial(factor_kernel, 1.0 / unit_total), in_spe...  20.3 us
    all_to_all x1, blocking collectives, body(): lax.all_to_all(mine.reshape(units, 1, share), 'unit', 0, 0, tiled=True)  17.4 us
    all_to_all x1, blocking collectives, body(): lax.all_to_all(spread_sum, 'unit', 0, 0, tiled=True).reshape(mine.shape)  16 us
    ppermute x3, waiting for transfers between devices, body(): row_parts[k] = lax.ppermute(outgoing[k], 'vec', around(parts, k))  10.5 us
    pallas_call x1, Pallas kernels, local_product(): pl.pallas_call(local_kernel, grid_spec=pltpu.PrefetchScalarGridSpec(num_s...  9.61 us
    ppermute x3, waiting for transfers between devices, body(): gathered[k] = lax.ppermute(quarter, 'vec', around(parts, k))  8.38 us
  transfers between devices with their start and end apart: 14, of which 10 were waited for; matrix products, arithmetic and copies ran while one was open for 0% of the time, Pallas kernels for 14%

profile of v5, /device:TPU:1, one launch (start us, length us, event | category | flops | bytes accessed | tf_op | source)
XLA Modules:
  0.0 215.8 jit_solution(14893834055393703428)
XLA Ops:
  0.6 2.1 spread_pieces.1
  2.8 44.3 %all_to_all.20.table_ref = bf16[64,72,128]{2,1,0:T(8,128)(2,1)S(1)} all-to-all(bf16[64,72,128]{2,1,0:T(8,128)(2,1)S(1)} %get-tuple-element.31), channel_id=1, replica_groups=mesh['unit'=64,'vec'=4] {'unit'}, dimensions={0} | all-to-all | bytes 2359296 | tf_op jit(solution)/shard_map/all_to_all | solution.py:482
  47.3 5.9 %pick_rows.1 = bf16[64,128,128]{2,1,0:T(8,128)(2,1)} custom-call(f32[2,16,128]{2,1,0:T(8,128)S(1)} %reshape.73.index_ref, bf16[64,72,128]{2,1,0:T(8,128)(2,1)S(1)} %all_to_all.20.table_ref), custom_call_target="tpu_custom_call" | custom-call | flops 4000000000 | bytes 4194304 | tf_op jit(solution)/shard_map/pick_rows/pallas_call | solution.py:177
  53.2 6.3 %all-to-all-start.1 = ((bf16[64,128,128]{2,1,0:T(8,128)(2,1)}), bf16[64,128,128]{2,1,0:T(8,128)(2,1)S(1)}, u32[]{:S(2)}, u32[]{:S(2)}) async-start(bf16[64,128,128]{2,1,0:T(8,128)(2,1)} %pick_rows.1), calls=%async_computation.1 | async-start | bytes 4194304 | tf_op jit(solution)/shard_map/all_to_all | solution.py:486
  59.6 3.4 %copy-done = bf16[256,128,128]{2,1,0:T(8,128)(2,1)S(1)} copy-done((bf16[256,128,128]{2,1,0:T(8,128)(2,1)S(1)}, bf16[256,128,128]{2,1,0:T(8,128)(2,1)}, u32[]{:S(2)}) %copy-start) | copy-done | bytes 8388632
  62.9 1.2 copy-done.3
  64.2 9.6 %local_blocks.1.acc_hbm = f32[32,128,128]{2,1,0:T(8,128)} custom-call(s32[256]{0:T(256)S(1)} %copy-done.4, s32[256]{0:T(256)S(1)} %copy-done.5, bf16[256,128,128]{2,1,0:T(8,128)(2,1)S(1)} %copy-done, bf16[32,128,128]{2,1,0:T(8,128)(2,1)S(1)} %copy-done.3, bf16[32,128,128]{2,1,0:T(8,128)(2,1)S(1)} %bitcast.20), custom_call_target="tpu_custom_call" | custom-call | flops 1073741824 | bytes 14680064 | tf_op jit(solution)/shard_map/local_blocks/pallas_call | solution.py:47
  73.8 37.0 %all-to-all-done.1.arrived_ref = bf16[64,128,128]{2,1,0:T(8,128)(2,1)S(1)} async-done(((bf16[64,128,128]{2,1,0:T(8,128)(2,1)}), bf16[64,128,128]{2,1,0:T(8,128)(2,1)S(1)}, u32[]{:S(2)}, u32[]{:S(2)}) %all-to-all-start.1) | async-done | bytes 2097184 | tf_op jit(solution)/shard_map/all_to_all | solution.py:486
  110.8 3.3 %far_blocks.1 = (bf16[32,128,128]{2,1,0:T(8,128)(2,1)S(1)}, bf16[16,128,128]{2,1,0:T(8,128)(2,1)S(1)}, bf16[16,128,128]{2,1,0:T(8,128)(2,1)S(1)}, bf16[8,128,128...) custom-call(s32[1]{0:T(128)} %bitcast.own_ref, ...), custom_call_target="tpu_custom_call" | custom-call | flops 268435456 | bytes 8388608 | tf_op jit(solution)/shard_map/far_blocks/pallas_call | solution.py:240
  114.1 1.3 collective-permute-start
  115.4 2.5 %collective-permute-start.1 = (bf16[8,128,128]{2,1,0:T(8,128)(2,1)S(1)}, bf16[8,128,128]{2,1,0:T(8,128)(2,1)S(1)}, u32[]{:S(2)}, u32[]{:S(2)}) collective-permute-start(bf16[8,128,128]{2,1,0:T(8,128)(2,1)S(1)} %get-tuple-element.35), channel_id=1, source_target_pairs={{0,2},{1,3},{2,0},{3,1},{4,6},{5,7},{6,4},{7,5},{8,10},{9,11},{10,... | collective-permute-start | bytes 786440 | tf_op jit(solution)/shard_map/ppermute | solution.py:496
  117.8 1.1 collective-permute-start.2
  119.0 3.9 %collective-permute-done = bf16[8,128,128]{2,1,0:T(8,128)(2,1)S(1)} collective-permute-done((bf16[8,128,128]{2,1,0:T(8,128)(2,1)S(1)}, bf16[8,128,128]{2,1,0:T(8,128)(2,1)S(1)}, u32[]{:S(2)}, u32[]{:S(2)}) %collective-permute-start) | collective-permute-done | bytes 262176 | tf_op jit(solution)/shard_map/ppermute | solution.py:496
  122.8 6.6 %collective-permute-done.1 = bf16[8,128,128]{2,1,0:T(8,128)(2,1)S(1)} collective-permute-done((bf16[8,128,128]{2,1,0:T(8,128)(2,1)S(1)}, bf16[8,128,128]{2,1,0:T(8,128)(2,1)S(1)}, u32[]{:S(2)}, u32[]{:S(2)}) %collective-permute-start.1) | collective-permute-done | bytes 262176 | tf_op jit(solution)/shard_map/ppermute | solution.py:496
  129.5 0.8 gram_quarters.1
  130.3 2.2 %collective-permute-start.3 = (f32[320,128]{1,0:T(8,128)S(1)}, f32[320,128]{1,0:T(8,128)S(1)}, u32[]{:S(2)}, u32[]{:S(2)}) collective-permute-start(f32[320,128]{1,0:T(8,128)S(1)} %get-tuple-element.38), channel_id=1, source_target_pairs={{0,2},{1,3},{2,0},{3,1},{4,6},{5,7},{6,4},{7,5},{8,10},{9,11},{10,... | collective-permute-start | bytes 491528 | tf_op jit(solution)/shard_map/ppermute | solution.py:501
  132.5 1.2 collective-permute-start.4
  133.7 1.5 collective-permute-start.5
  135.2 0.9 collective-permute-done.3
  136.0 4.4 %collective-permute-done.4 = f32[320,128]{1,0:T(8,128)S(1)} collective-permute-done((f32[320,128]{1,0:T(8,128)S(1)}, f32[320,128]{1,0:T(8,128)S(1)}, u32[]{:S(2)}, u32[]{:S(2)}) %collective-permute-start.4) | collective-permute-done | bytes 163872 | tf_op jit(solution)/shard_map/ppermute | solution.py:501
  141.0 2.5 %collective-permute-start.7 = (bf16[32,128,128]{2,1,0:T(8,128)(2,1)S(1)}, bf16[32,128,128]{2,1,0:T(8,128)(2,1)S(1)}, u32[]{:S(2)}, u32[]{:S(2)}) collective-permute-start(bf16[32,128,128]{2,1,0:T(8,128)(2,1)S(1)} %get-tuple-element.41), channel_id=1, source_target_pairs={{0,3},{1,0},{2,1},{3,2},{4,7},{5,4},{6,5},{7,6},{8,11},{9,8},{10,9... | collective-permute-start | bytes 3145736 | tf_op jit(solution)/shard_map/ppermute | solution.py:504
  143.5 17.4 %all_to_all.21 = f32[64,1,640]{2,1,0:T(1,128)S(1)} all-to-all(f32[64,1,640]{2,1,0:T(1,128)S(1)} %bitcast.33), channel_id=1, replica_groups=mesh['unit'=64,'vec'=4] {'unit'}, dimensions={0} | all-to-all | bytes 327680 | tf_op jit(solution)/shard_map/all_to_all | solution.py:507
  161.1 1.4 collective-permute-start.8
  162.6 16.0 %all_to_all.22 = f32[64,1,640]{2,1,0:T(1,128)S(1)} all-to-all(f32[64,1,640]{2,1,0:T(1,128)S(1)} %broadcast_in_dim.12), channel_id=1, replica_groups=mesh['unit'=64,'vec'=4] {'unit'}, dimensions={0} | all-to-all | bytes 327680 | tf_op jit(solution)/shard_map/all_to_all | solution.py:512
  178.9 1.5 collective-permute-start.11
  180.4 2.3 %collective-permute-start.10 = (f32[320,128]{1,0:T(8,128)S(1)}, f32[320,128]{1,0:T(8,128)S(1)}, u32[]{:S(2)}, u32[]{:S(2)}) collective-permute-start(f32[320,128]{1,0:T(8,128)S(1)} %bitcast.26), channel_id=1, source_target_pairs={{0,2},{1,3},{2,0},{3,1},{4,6},{5,7},{6,4},{7,5},{8,10},{9,11},{10,... | collective-permute-start | bytes 491528 | tf_op jit(solution)/shard_map/ppermute | solution.py:516
  182.7 0.9 collective-permute-done.11.refs_3_
  183.7 2.5 %collective-permute-done.10.refs_2_ = f32[320,128]{1,0:T(8,128)S(1)} collective-permute-done((f32[320,128]{1,0:T(8,128)S(1)}, f32[320,128]{1,0:T(8,128)S(1)}, u32[]{:S(2)}, u32[]{:S(2)}) %collective-permute-start.10) | collective-permute-done | bytes 163872 | tf_op jit(solution)/shard_map/ppermute | solution.py:516
  186.1 5.0 %collective-permute-done.9.refs_1_ = f32[320,128]{1,0:T(8,128)S(1)} collective-permute-done((f32[320,128]{1,0:T(8,128)S(1)}, f32[320,128]{1,0:T(8,128)S(1)}, u32[]{:S(2)}, u32[]{:S(2)}) %collective-permute-start.9) | collective-permute-done | bytes 163872 | tf_op jit(solution)/shard_map/ppermute | solution.py:516
  191.1 1.0 collective-permute-start.12
  192.1 20.3 %factor.1 = (bf16[4,4,128,128]{3,2,1,0:T(8,128)(2,1)S(1)}, f32[4,128]{1,0:T(4,128)}) custom-call(s32[1]{0:T(128)} %bitcast.own_ref, f32[320,128]{1,0:T(8,128)S(1)} %bitcast.28, f32[320,128]{1,0:T(8,128)S(1)} %collective-permute-done.9.refs_1_, f32[320,128]{1,0:T(8,128)S(1)} %collective-permute-done.10.refs_2_, f32[320,128]{1,0:T(8,128)S(1)} %collective-permute-done.11.refs_3_), custom_call_target="tpu_custom_call" | custom-call | flops 200000000 | bytes 2097152 | tf_op jit(solution)/shard_map/factor/pallas_call | solution.py:391
  212.5 3.1 %renew.1 = bf16[4096,128]{1,0:T(8,128)(2,1)} custom-call(s32[1]{0:T(128)} %bitcast.own_ref, bf16[4096,128]{1,0:T(8,128)(2,1)S(1)} %bitcast.21, bf16[4096,128]{1,0:T(8,128)(2,1)S(1)} %bitcast.23, bf16[2048,128]{1,0:T(8,128)(2,1)} %bitcast.15.near2, bf16[2048,128]{1,0:T(8,128)(2,1)S(1)} %bitcast.24, bf16[4096,128]{1,0:T(8,128)(2,1)S(1)} %bitcast.22, ...), custom_call_target="tpu_custom_call" | custom-call | flops 536870912 | bytes 6291456 | tf_op jit(solution)/shard_map/renew/pallas_call | solution.py:438
  (32 shorter events, 1.3 us)
Async XLA Ops:
  2.8 44.3 %copy-start.2 = (bf16[32,128,128]{2,1,0:T(8,128)(2,1)}, bf16[32,128,128]{2,1,0:T(8,128)(2,1)S(1)}, u32[]{:S(2)}) copy-start(bf16[32,128,128]{2,1,0:T(8,128)(2,1)S(1)} %get-tuple-element.30.x_ref) | copy-start | bytes 3145732
  53.2 6.3 %copy-start.1 = (bf16[4096,128]{1,0:T(8,128)(2,1)S(1)}, bf16[4096,128]{1,0:T(8,128)(2,1)}, u32[]{:S(2)}) copy-start(bf16[4096,128]{1,0:T(8,128)(2,1)} %param.10) | copy-start | bytes 3145732
  53.2 6.3 %copy-start.4 = (s32[256]{0:T(256)S(1)}, s32[256]{0:T(256)}, u32[]{:S(2)}) copy-start(s32[256]{0:T(256)} %row_ref.2) | copy-start | bytes 3076
  53.2 6.4 %copy-start.5 = (s32[256]{0:T(256)S(1)}, s32[256]{0:T(256)}, u32[]{:S(2)}) copy-start(s32[256]{0:T(256)} %col_ref.1) | copy-start | bytes 3076
  53.2 57.6 %all-to-all-start.1 = ((bf16[64,128,128]{2,1,0:T(8,128)(2,1)}), bf16[64,128,128]{2,1,0:T(8,128)(2,1)S(1)}, u32[]{:S(2)}, u32[]{:S(2)}) async-start(bf16[64,128,128]{2,1,0:T(8,128)(2,1)} %pick_rows.1), calls=%async_computation.1 | async-start | bytes 4194304 | tf_op jit(solution)/shard_map/all_to_all | solution.py:486
  59.5 3.4 %copy-start = (bf16[256,128,128]{2,1,0:T(8,128)(2,1)S(1)}, bf16[256,128,128]{2,1,0:T(8,128)(2,1)}, u32[]{:S(2)}) copy-start(bf16[256,128,128]{2,1,0:T(8,128)(2,1)} %w_ref.1) | copy-start | bytes 25165828
  62.9 1.2 copy-start.3
  64.2 46.6 %copy-start.6 = (s32[64]{0:T(128)S(1)}, s32[64]{0:T(128)}, u32[]{:S(2)}) copy-start(s32[64]{0:T(128)} %row_ref.3) | copy-start | bytes 772
  114.0 27.0 %copy-start.7 = (bf16[16,128,128]{2,1,0:T(8,128)(2,1)}, bf16[16,128,128]{2,1,0:T(8,128)(2,1)S(1)}, u32[]{:S(2)}) copy-start(bf16[16,128,128]{2,1,0:T(8,128)(2,1)S(1)} %get-tuple-element.50) | copy-start | bytes 1572868
  114.1 29.5 %copy-start.8 = (bf16[16,128,128]{2,1,0:T(8,128)(2,1)}, bf16[16,128,128]{2,1,0:T(8,128)(2,1)S(1)}, u32[]{:S(2)}) copy-start(bf16[16,128,128]{2,1,0:T(8,128)(2,1)S(1)} %get-tuple-element.45) | copy-start | bytes 1572868
  114.1 8.8 %collective-permute-start = (bf16[8,128,128]{2,1,0:T(8,128)(2,1)S(1)}, bf16[8,128,128]{2,1,0:T(8,128)(2,1)S(1)}, u32[]{:S(2)}, u32[]{:S(2)}) collective-permute-start(bf16[8,128,128]{2,1,0:T(8,128)(2,1)S(1)} %get-tuple-element.34), channel_id=1, source_target_pairs={{0,1},{1,2},{2,3},{3,0},{4,5},{5,6},{6,7},{7,4},{8,9},{9,10},{10,1... | collective-permute-start | bytes 786440 | tf_op jit(solution)/shard_map/ppermute | solution.py:496
  115.4 14.1 %collective-permute-start.1 = (bf16[8,128,128]{2,1,0:T(8,128)(2,1)S(1)}, bf16[8,128,128]{2,1,0:T(8,128)(2,1)S(1)}, u32[]{:S(2)}, u32[]{:S(2)}) collective-permute-start(bf16[8,128,128]{2,1,0:T(8,128)(2,1)S(1)} %get-tuple-element.35), channel_id=1, source_target_pairs={{0,2},{1,3},{2,0},{3,1},{4,6},{5,7},{6,4},{7,5},{8,10},{9,11},{10,... | collective-permute-start | bytes 786440 | tf_op jit(solution)/shard_map/ppermute | solution.py:496
  117.8 11.6 %collective-permute-start.2 = (bf16[8,128,128]{2,1,0:T(8,128)(2,1)S(1)}, bf16[8,128,128]{2,1,0:T(8,128)(2,1)S(1)}, u32[]{:S(2)}, u32[]{:S(2)}) collective-permute-start(bf16[8,128,128]{2,1,0:T(8,128)(2,1)S(1)} %get-tuple-element.36), channel_id=1, source_target_pairs={{0,3},{1,0},{2,1},{3,2},{4,7},{5,4},{6,5},{7,6},{8,11},{9,8},{10,9... | collective-permute-start | bytes 786440 | tf_op jit(solution)/shard_map/ppermute | solution.py:496
  130.3 5.8 %collective-permute-start.3 = (f32[320,128]{1,0:T(8,128)S(1)}, f32[320,128]{1,0:T(8,128)S(1)}, u32[]{:S(2)}, u32[]{:S(2)}) collective-permute-start(f32[320,128]{1,0:T(8,128)S(1)} %get-tuple-element.38), channel_id=1, source_target_pairs={{0,2},{1,3},{2,0},{3,1},{4,6},{5,7},{6,4},{7,5},{8,10},{9,11},{10,... | collective-permute-start | bytes 491528 | tf_op jit(solution)/shard_map/ppermute | solution.py:501
  132.5 8.0 %collective-permute-start.4 = (f32[320,128]{1,0:T(8,128)S(1)}, f32[320,128]{1,0:T(8,128)S(1)}, u32[]{:S(2)}, u32[]{:S(2)}) collective-permute-start(f32[320,128]{1,0:T(8,128)S(1)} %get-tuple-element.39), channel_id=1, source_target_pairs={{0,1},{1,2},{2,3},{3,0},{4,5},{5,6},{6,7},{7,4},{8,9},{9,10},{10,1... | collective-permute-start | bytes 491528 | tf_op jit(solution)/shard_map/ppermute | solution.py:501
  133.7 7.3 %collective-permute-start.5 = (f32[320,128]{1,0:T(8,128)S(1)}, f32[320,128]{1,0:T(8,128)S(1)}, u32[]{:S(2)}, u32[]{:S(2)}) collective-permute-start(f32[320,128]{1,0:T(8,128)S(1)} %get-tuple-element.40), channel_id=1, source_target_pairs={{0,3},{1,0},{2,1},{3,2},{4,7},{5,4},{6,5},{7,6},{8,11},{9,8},{10,9... | collective-permute-start | bytes 491528 | tf_op jit(solution)/shard_map/ppermute | solution.py:501
  141.0 37.9 %collective-permute-start.7 = (bf16[32,128,128]{2,1,0:T(8,128)(2,1)S(1)}, bf16[32,128,128]{2,1,0:T(8,128)(2,1)S(1)}, u32[]{:S(2)}, u32[]{:S(2)}) collective-permute-start(bf16[32,128,128]{2,1,0:T(8,128)(2,1)S(1)} %get-tuple-element.41), channel_id=1, source_target_pairs={{0,3},{1,0},{2,1},{3,2},{4,7},{5,4},{6,5},{7,6},{8,11},{9,8},{10,9... | collective-permute-start | bytes 3145736 | tf_op jit(solution)/shard_map/ppermute | solution.py:504
  143.5 35.4 %collective-permute-start.6 = (bf16[32,128,128]{2,1,0:T(8,128)(2,1)S(1)}, bf16[32,128,128]{2,1,0:T(8,128)(2,1)S(1)}, u32[]{:S(2)}, u32[]{:S(2)}) collective-permute-start(bf16[32,128,128]{2,1,0:T(8,128)(2,1)S(1)} %get-tuple-element.41), channel_id=1, source_target_pairs={{0,1},{1,2},{2,3},{3,0},{4,5},{5,6},{6,7},{7,4},{8,9},{9,10},{10,1... | collective-permute-start | bytes 3145736 | tf_op jit(solution)/shard_map/ppermute | solution.py:504
  161.1 17.8 %collective-permute-start.8 = (bf16[16,128,128]{2,1,0:T(8,128)(2,1)}, bf16[16,128,128]{2,1,0:T(8,128)(2,1)}, u32[]{:S(2)}, u32[]{:S(2)}) collective-permute-start(bf16[16,128,128]{2,1,0:T(8,128)(2,1)} %copy-done.8), channel_id=1, source_target_pairs={{0,2},{1,3},{2,0},{3,1},{4,6},{5,7},{6,4},{7,5},{8,10},{9,11},{10,... | collective-permute-start | bytes 1572872 | tf_op jit(solution)/shard_map/ppermute | solution.py:510
  178.9 4.8 %collective-permute-start.11 = (f32[320,128]{1,0:T(8,128)S(1)}, f32[320,128]{1,0:T(8,128)S(1)}, u32[]{:S(2)}, u32[]{:S(2)}) collective-permute-start(f32[320,128]{1,0:T(8,128)S(1)} %bitcast.25), channel_id=1, source_target_pairs={{0,3},{1,0},{2,1},{3,2},{4,7},{5,4},{6,5},{7,6},{8,11},{9,8},{10,9... | collective-permute-start | bytes 491528 | tf_op jit(solution)/shard_map/ppermute | solution.py:516
  180.4 5.7 %collective-permute-start.10 = (f32[320,128]{1,0:T(8,128)S(1)}, f32[320,128]{1,0:T(8,128)S(1)}, u32[]{:S(2)}, u32[]{:S(2)}) collective-permute-start(f32[320,128]{1,0:T(8,128)S(1)} %bitcast.26), channel_id=1, source_target_pairs={{0,2},{1,3},{2,0},{3,1},{4,6},{5,7},{6,4},{7,5},{8,10},{9,11},{10,... | collective-permute-start | bytes 491528 | tf_op jit(solution)/shard_map/ppermute | solution.py:516
  182.7 8.4 %collective-permute-start.9 = (f32[320,128]{1,0:T(8,128)S(1)}, f32[320,128]{1,0:T(8,128)S(1)}, u32[]{:S(2)}, u32[]{:S(2)}) collective-permute-start(f32[320,128]{1,0:T(8,128)S(1)} %bitcast.27), channel_id=1, source_target_pairs={{0,1},{1,2},{2,3},{3,0},{4,5},{5,6},{6,7},{7,4},{8,9},{9,10},{10,1... | collective-permute-start | bytes 491528 | tf_op jit(solution)/shard_map/ppermute | solution.py:516
  191.1 21.3 %collective-permute-start.12 = (bf16[16,128,128]{2,1,0:T(8,128)(2,1)}, bf16[16,128,128]{2,1,0:T(8,128)(2,1)S(1)}, u32[]{:S(2)}, u32[]{:S(2)}) collective-permute-start(bf16[16,128,128]{2,1,0:T(8,128)(2,1)} %copy-done.7), channel_id=1, source_target_pairs={{0,2},{1,3},{2,0},{3,1},{4,6},{5,7},{6,4},{7,5},{8,10},{9,11},{10,... | collective-permute-start | bytes 1572872 | tf_op jit(solution)/shard_map/ppermute | solution.py:519
